TPU v7x, 256 devices: a whole 4x4x8 slice. The times are simulated.
256 devices in a mesh: inner: 32 (over z_hi, x, y), outer: 8 (over z_lo, core).
Axes of the slice: x: 4, y: 4, z: 8 (z_hi: 2, z_lo: 4; z = z_hi * 4 + z_lo), core: 2. Of those that a mesh axis runs over, the one named last changes fastest.
Arguments:
- queries: bfloat16 [131072, 8, 128], P(('inner', 'outer')), may hold values from -6 to 6
- key_tokens: bfloat16 [131072, 128], P(('inner', 'outer')), may hold values from -6 to 6
- value_tokens: bfloat16 [131072, 128], P(('inner', 'outer')), may hold values from -6 to 6
- out_grad: bfloat16 [131072, 8, 128], P(('inner', 'outer')), may hold values from -4 to 4
- forward_out: bfloat16 [131072, 8, 128], P(('inner', 'outer')), may hold values from -4 to 4
- log_norm: float32 [131072, 8], P(('inner', 'outer')), may hold values from 2 to 5
- block_list: int32 [1024, 8], P(('inner', 'outer')), may hold values from 0 to 1023, as said below
- block_live: int32 [1024], P(('inner', 'outer')), may hold values from 1 to 8
Outputs:
- query_grad: bfloat16 [131072, 8, 128], P(('inner', 'outer'))
- key_grad: bfloat16 [131072, 128], P(('inner', 'outer'))
- value_grad: bfloat16 [131072, 128], P(('inner', 'outer'))
Inputs may be any that keep to these rules, and one draw needn't show every extreme that they name: `block_list`: for query block b the first block_live[b] entries are distinct key block numbers k <= b, always including b itself, with k lying in the tokens of the device that holds b or of the 4 devices before it along inner+outer; the remaining entries equal b. Some query block uses all 8 entries.
All inputs are finite; a program needn't handle non-finite values.
Results may differ from a plain program's by a relative error of at most 0.0056.
Values may be sent and summed in bfloat16 or wider, within the bound.
No kernel may reach another device: no remote copies, remote signals or barrier semaphores. Data moves between devices by JAX's collectives and lax.ppermute only.
A program may use at most 64 MiB of HBM per device.

v0:
```python
import functools

import jax
import jax.numpy as jnp
from jax import lax
from jax.experimental import pallas as pl
from jax.experimental.pallas import tpu as pltpu
from jax.sharding import PartitionSpec as P

BLOCK = 128
CODE_BITS = 4
CODES = 1 << CODE_BITS
SPARE = 384
AXES = ("inner", "outer")
LOG2E = 1.4426950408889634
NT = (((1,), (1,)), ((), ()))
TN = (((0,), (0,)), ((), ()))
F32 = jnp.float32
BF16 = jnp.bfloat16


def ring_shift(block, distance):
    count = lax.axis_size(AXES)
    route = [(i, (i + distance) % count) for i in range(count)]
    return lax.ppermute(block, AXES, route)


def pair_swap(block):
    count = lax.axis_size(AXES)
    return lax.ppermute(block, AXES, [(i, i ^ 1) for i in range(count)])


def tile_terms(keys, values, qrows, grows, norm, delta, scale, mask=None):
    score = lax.dot_general(keys, qrows, NT, preferred_element_type=F32)
    dweight = lax.dot_general(values, grows, NT, preferred_element_type=F32)
    weight = jnp.exp2(score * (scale * LOG2E) - norm)
    if mask is not None:
        weight = jnp.where(mask, weight, 0.0)
    score_grad = (weight * (dweight - delta)).astype(BF16)
    value_part = jnp.dot(weight.astype(BF16), grows, preferred_element_type=F32)
    key_part = jnp.dot(score_grad, qrows, preferred_element_type=F32)
    query_part = lax.dot_general(keys, score_grad, TN, preferred_element_type=F32)
    return query_part, key_part, value_part


def block_rows(index, size):
    return pl.ds(pl.multiple_of(index * size, size), size)


def own_place(position, shard):
    return shard == position, 0


def near_place(position, shard):
    back = (position >> 1) - (shard >> 1)
    other = (position ^ shard) & 1
    return (back == 1) | ((back == 0) & (other == 1)), back + (back & other)


def far_place(position, shard):
    back = (position >> 1) - (shard >> 1)
    return back == 2, (position ^ shard) & 1


def listed_items(position, list_ref, live_ref, items_ref, place_of, shards):
    local_blocks, slots = list_ref.shape
    shift = local_blocks.bit_length() - 1
    doubles, singles = jnp.int32(0), jnp.int32(0)
    for step in range(local_blocks):

        def one(slot, carry, step=step):
            doubles, waiting, last = carry
            block = list_ref[step, slot]
            keep, place = place_of(position, block >> shift)
            keep = (keep & (block != position * local_blocks + step)).astype(jnp.int32)
            local = place * local_blocks + (block & (local_blocks - 1))
            code = step * CODES + local
            items_ref[0, doubles] = last * CODES * CODES + code
            doubles = doubles + (keep & waiting)
            return doubles, keep ^ waiting, jnp.where(keep == 1, code, last)

        doubles, waiting, last = lax.fori_loop(
            0, live_ref[step], one, (doubles, jnp.int32(0), jnp.int32(0))
        )
        items_ref[1, singles] = last
        singles = singles + waiting
    return doubles, singles


def run_items(counts, items_ref, k_ref, v_ref, q_ref, g_ref, norm_ref, delta_ref,
              dq_ref, dk_ref, dv_ref, scale):
    rows = norm_ref.shape[2]

    def some(row, start, number):
        entries = []
        for offset in range(number):
            item = items_ref[row, start + offset]
            places = [item & (CODES - 1)]
            if row == 0:
                places.append((item >> (2 * CODE_BITS)) & (CODES - 1))
            entries.append(((item >> CODE_BITS) & (CODES - 1), [block_rows(p, BLOCK) for p in places]))
        terms = []
        for step, spans in entries:
            span = block_rows(step, rows)
            keys = jnp.concatenate([k_ref[at, :] for at in spans], axis=0)
            values = jnp.concatenate([v_ref[at, :] for at in spans], axis=0)
            terms.append(
                tile_terms(
                    keys, values, q_ref[span, :], g_ref[span, :], norm_ref[step], delta_ref[step],
                    scale,
                )
            )
        for (step, spans), (dq, dk, dv) in zip(entries, terms):
            dq_ref[step] += dq
            for index, at in enumerate(spans):
                part = slice(index * BLOCK, (index + 1) * BLOCK)
                dk_ref[at, :] += dk[part]
                dv_ref[at, :] += dv[part]

    for row, count in enumerate(counts):

        def two(index, carry, row=row):
            some(row, index * 2, 2)
            return carry

        lax.fori_loop(0, count // 2, two, 0)

        @pl.when(count % 2 == 1)
        def _(row=row, count=count):
            some(row, count - 1, 1)


def own_kernel(
    position_ref, list_hbm, live_hbm, q_hbm, g_hbm, o_hbm, norm_hbm, k_hbm, v_hbm,
    list_out, live_out, q_ref, g_ref, norm_ref, delta_ref, dq_ref, dk_ref, dv_ref, both_ref,
    o_ref, raw_ref, list_ref, live_ref, items_ref, row_sems, sems, *, scale,
):
    local_blocks = list_ref.shape[0]
    head_size = q_ref.shape[1]
    rows = norm_ref.shape[2]
    heads = rows // BLOCK
    tokens = local_blocks * BLOCK
    k_ref, v_ref = both_ref.at[pl.ds(0, tokens), :], both_ref.at[pl.ds(tokens, tokens), :]
    single = [
        pltpu.make_async_copy(source, target, sems.at[index])
        for index, (source, target) in enumerate(
            (
                (norm_hbm, raw_ref), (k_hbm, k_ref), (v_hbm, v_ref), (list_hbm, list_ref),
                (live_hbm, live_ref), (list_hbm, list_out), (live_hbm, live_out),
            )
        )
    ]
    moves = []
    for step in range(local_blocks):
        span = pl.ds(step * rows, rows)
        moves.append([
            pltpu.make_async_copy(source.at[span, :], target.at[span, :], row_sems.at[index, step])
            for index, (source, target) in enumerate(
                ((g_hbm, g_ref), (o_hbm, o_ref), (q_hbm, q_ref))
            )
        ])
    for copy in moves[0] + single + moves[1] + moves[2] + moves[3]:
        copy.start()
    ones = jnp.ones((8, 2 * head_size), BF16)
    key_pos = lax.broadcasted_iota(jnp.int32, (BLOCK, rows), 0)
    row_pos = lax.broadcasted_iota(jnp.int32, (BLOCK, rows), 1)
    mask = key_pos * heads <= row_pos
    same_token = jnp.where(key_pos == row_pos // heads, 1.0, 0.0).astype(BF16)
    head_pos = lax.broadcasted_iota(jnp.int32, (3 * heads, rows), 0) % heads
    same_head = head_pos == lax.broadcasted_iota(jnp.int32, (3 * heads, rows), 1) % heads
    for copy in single:
        copy.wait()
    for step in range(local_blocks):
        span = pl.ds(step * rows, rows)
        at = pl.ds(step * BLOCK, BLOCK)
        rest = raw_ref[:, at] * LOG2E
        pieces = []
        for _ in range(3):
            pieces.append(rest.astype(BF16).astype(F32))
            rest = rest - pieces[-1]
        pieces = jnp.concatenate(pieces, axis=0).astype(BF16)
        spread = jnp.dot(pieces, same_token, preferred_element_type=F32)
        norm = jnp.sum(jnp.where(same_head, spread, 0.0), axis=0, keepdims=True)
        norm_ref[step] = norm
        for copy in moves[step]:
            copy.wait()
        product = g_ref[span, :].astype(F32) * o_ref[span, :].astype(F32)
        high = product.astype(BF16)
        low = (product - high.astype(F32)).astype(BF16)
        both = jnp.concatenate([high, low], axis=1)
        delta = lax.dot_general(ones, both, NT, preferred_element_type=F32)
        delta_ref[step] = delta[:1]
        dq, dk, dv = tile_terms(
            k_ref[at, :], v_ref[at, :], q_ref[span, :], g_ref[span, :], norm, delta[:1], scale, mask
        )
        dq_ref[step] = dq
        dk_ref[at, :] = dk
        dv_ref[at, :] = dv
    counts = listed_items(position_ref[0], list_ref, live_ref, items_ref, own_place, 1)
    run_items(
        counts, items_ref, k_ref, v_ref, q_ref, g_ref, norm_ref, delta_ref,
        dq_ref, dk_ref, dv_ref, scale,
    )
    dk_ref[...] = dk_ref[...] * scale


def shards_kernel(position_ref, list_ref, live_ref, q_ref, g_ref, norm_ref, delta_ref, *refs,
                  scale, parts, shards, place_of):
    tokens = list_ref.shape[0] * BLOCK
    inputs = []
    for ref in refs[1 : 1 + parts]:
        inputs += [ref.at[pl.ds(start, tokens), :] for start in range(0, ref.shape[0], tokens)]
    dq_ref = refs[1 + parts]
    outs = refs[2 + parts : -5]
    k_all, v_all, dk_acc, dv_acc, items_ref = refs[-5:]
    counts = listed_items(position_ref[0], list_ref, live_ref, items_ref, place_of, shards)
    for index in range(shards):
        span = pl.ds(index * tokens, tokens)
        k_all[span, :] = inputs[2 * index][...]
        v_all[span, :] = inputs[2 * index + 1][...]
    dk_acc[...] = jnp.zeros_like(dk_acc)
    dv_acc[...] = jnp.zeros_like(dv_acc)
    run_items(
        counts, items_ref, k_all, v_all, q_ref, g_ref, norm_ref,
        delta_ref, dq_ref, dk_acc, dv_acc, scale,
    )
    pieces = len(outs) - shards + 1
    size = 2 * tokens // pieces
    for index in range(pieces // 2):
        span = pl.ds((shards - 1) * tokens + index * size, size)
        outs[index][...] = (dk_acc[span, :] * scale).astype(BF16)
        outs[pieces // 2 + index][...] = dv_acc[span, :].astype(BF16)
    for ref, place in zip(outs[pieces:], range(shards - 2, -1, -1)):
        span = pl.ds(place * tokens, tokens)
        ref[pl.ds(0, tokens), :] = (dk_acc[span, :] * scale).astype(BF16)
        ref[pl.ds(tokens, tokens), :] = dv_acc[span, :].astype(BF16)


def add_kernel(straight_ref, *refs, outs):
    crossed, out_refs = refs[:-outs], refs[-outs:]
    size = crossed[0].shape[0]
    whole = len(crossed) * size // outs
    for index, ref in enumerate(crossed):
        span = pl.ds(index * size, size)
        out_span = pl.ds(index * size % whole, size)
        total = straight_ref[span, :].astype(F32) + ref[...].astype(F32)
        out_refs[index * size // whole][out_span, :] = total.astype(BF16)
    if outs == 1:
        span = pl.ds(whole, SPARE)
        out_refs[0][span, :] = jnp.zeros((SPARE, straight_ref.shape[1]), BF16)


def finish_kernel(dq_ref, out_ref, *, scale):
    out_ref[...] = (dq_ref[0] * scale).T.astype(out_ref.dtype)


def in_vmem(array):
    return pltpu.with_memory_space_constraint(array, pltpu.VMEM)


def in_hbm(array):
    return pltpu.with_memory_space_constraint(array, pltpu.HBM)


def body(
    queries, key_tokens, value_tokens, out_grad, forward_out, log_norm, block_list, block_live
):
    local_tokens, heads, head_size = queries.shape
    local_blocks, slots = block_list.shape
    rows = BLOCK * heads
    all_rows = (local_blocks * rows, head_size)
    scale = head_size ** (-0.5)
    position = lax.axis_index(AXES).astype(jnp.int32)
    device = position.reshape(1)

    smem = pl.BlockSpec(memory_space=pltpu.SMEM)
    vmem = pl.BlockSpec(memory_space=pltpu.VMEM)
    anywhere = pl.BlockSpec(memory_space=pl.ANY)
    line_shape = pltpu.VMEM((local_blocks, 1, rows), F32)
    rows_shape = pltpu.VMEM(all_rows, BF16)
    dq_shape = pltpu.VMEM((local_blocks, head_size, rows), F32)
    wide_shape = jax.ShapeDtypeStruct((local_tokens, head_size), F32)
    spare_shape = jax.ShapeDtypeStruct((2 * local_tokens + SPARE, head_size), BF16)
    quarter = jax.ShapeDtypeStruct((local_tokens // 2, head_size), BF16)
    items = pltpu.SMEM((2, local_blocks * slots + 1), jnp.int32)
    params = pltpu.CompilerParams(vmem_limit_bytes=24 * 1024 * 1024)

    def stacked(number):
        return jax.ShapeDtypeStruct((number * local_tokens, head_size), BF16)

    def cost(slots):
        return pl.CostEstimate(flops=slots, bytes_accessed=slots, transcendentals=0)

    def own_call():
        outs = pl.pallas_call(
            functools.partial(own_kernel, scale=scale),
            in_specs=[smem] + [anywhere] * 8,
            out_specs=[vmem] * 10,
            out_shape=[pltpu.VMEM(block_list.shape, jnp.int32)]
            + [pltpu.VMEM(block_live.shape, jnp.int32)]
            + [rows_shape] * 2 + [line_shape] * 2 + [dq_shape] + [wide_shape] * 2 + [stacked(2)],
            scratch_shapes=[
                pltpu.VMEM(all_rows, BF16), pltpu.VMEM((heads, local_tokens), F32),
                pltpu.SMEM(block_list.shape, jnp.int32), pltpu.SMEM(block_live.shape, jnp.int32),
                items, pltpu.SemaphoreType.DMA((3, local_blocks)), pltpu.SemaphoreType.DMA((7,)),
            ],
            compiler_params=params,
            cost_estimate=cost(1),
            name="own_shard",
        )(
            device, in_hbm(block_list), in_hbm(block_live),
            in_hbm(queries.reshape(all_rows)), in_hbm(out_grad.reshape(all_rows)),
            in_hbm(forward_out.reshape(all_rows)), in_hbm(log_norm.T),
            in_hbm(key_tokens), in_hbm(value_tokens),
        )
        return [in_vmem(x) for x in outs[:7]] + list(outs[7:])

    def shards_call(dq, parts, shards, place_of, name):
        wide = pltpu.VMEM((shards * local_tokens, head_size), F32)
        narrow = pltpu.VMEM((shards * local_tokens, head_size), BF16)
        return pl.pallas_call(
            functools.partial(
                shards_kernel, scale=scale, parts=len(parts), shards=shards, place_of=place_of
            ),
            in_specs=[smem] * 3 + [vmem] * (5 + len(parts)),
            out_specs=[vmem] * (shards + (4 if shards == 3 else 2)),
            out_shape=[dq_shape]
            + ([quarter] * 4 if shards == 3 else [stacked(1)] * 2)
            + [stacked(2)] * (shards - 1),
            scratch_shapes=[narrow, narrow, wide, wide, items],
            input_output_aliases={7: 0},
            compiler_params=params,
            cost_estimate=cost(1),
            name=name,
        )(device, listed, live, q, g, norm, delta, in_vmem(dq), *map(in_vmem, parts))

    def add_call(straight, crossed, shapes, name):
        return pl.pallas_call(
            functools.partial(add_kernel, outs=len(shapes)),
            in_specs=[vmem] * (1 + len(crossed)),
            out_specs=[vmem] * len(shapes),
            out_shape=shapes,
            compiler_params=params,
            cost_estimate=cost(1),
            name=name,
        )(*map(in_vmem, (straight, *crossed)))

    def finish_call(dq):
        return pl.pallas_call(
            functools.partial(finish_kernel, scale=scale),
            grid=(local_blocks,),
            in_specs=[pl.BlockSpec((1, head_size, rows), lambda i: (i, 0, 0))],
            out_specs=pl.BlockSpec((rows, head_size), lambda i: (i, 0)),
            out_shape=jax.ShapeDtypeStruct(all_rows, BF16),
            compiler_params=params,
            cost_estimate=cost(1),
            name="query_grad",
        )(in_vmem(dq))

    k2, v2 = ring_shift(key_tokens, 2), ring_shift(value_tokens, 2)
    listed, live, q, g, norm, delta, dq, dk0, dv0, kv = own_call()
    k2, v2, kv, dq = lax.optimization_barrier((k2, v2, kv, dq))
    k4, v4 = ring_shift(k2, 2), ring_shift(v2, 2)
    dq, *crossed, near, other = shards_call(
        dq, (pair_swap(kv), k2, v2, pair_swap(k2), pair_swap(v2)), 3, near_place, "near_shards"
    )
    (near,) = add_call(near, [pair_swap(x) for x in crossed], [spare_shape], "near_sum")
    near = ring_shift(near, -2)
    k4, v4, dq = lax.optimization_barrier((k4, v4, dq))
    dq, *crossed, far = shards_call(
        dq, (k4, v4, pair_swap(k4), pair_swap(v4)), 2, far_place, "far_shards"
    )
    far = add_call(far, [pair_swap(x) for x in crossed], [stacked(1)] * 2, "far_sum")
    far_k, far_v = (ring_shift(part, -4) for part in far)
    near, dq = lax.optimization_barrier((near, dq))
    query_grad = finish_call(dq)
    far_k, far_v, query_grad = lax.optimization_barrier((far_k, far_v, query_grad))
    rest = pair_swap(other).astype(F32) + near[: 2 * local_tokens].astype(F32)
    key_grad = (dk0 + rest[:local_tokens] + far_k.astype(F32)).astype(BF16)
    value_grad = (dv0 + rest[local_tokens:] + far_v.astype(F32)).astype(BF16)
    return query_grad.reshape(queries.shape), key_grad, value_grad


def solution(mesh):
    tokens = P(AXES, None)
    wide = P(AXES, None, None)
    return jax.shard_map(
        body,
        mesh=mesh,
        in_specs=(wide, tokens, tokens, wide, wide, tokens, tokens, P(AXES)),
        out_specs=(wide, tokens, tokens),
        check_vma=False,
    )
```

profile of v0, /device:TPU:126, one launch (start us, length us, event | category | flops | bytes accessed | tf_op | source)
XLA Modules:
  0.0 54.3 jit_solution(5146456671113355435)
XLA Ops:
  0.6 2.8 %collective-permute-start = (bf16[512,128]{1,0:T(8,128)(2,1)}, bf16[512,128]{1,0:T(8,128)(2,1)S(1)}, u32[]{:S(2)}, u32[]{:S(2)}) collective-permute-start(bf16[512,128]{1,0:T(8,128)(2,1)} %k_hbm.1), channel_id=1, source_target_pairs={{0,2},{1,3},{2,4},{3,5},{4,6},{5,7},{6,8},{7,9},{8,10},{9,11},{10,... | collective-permute-start | bytes 393224 | tf_op jit(solution)/shard_map/ppermute | solution.py:25
  3.4 1.0 %collective-permute-start.1 = (bf16[512,128]{1,0:T(8,128)(2,1)}, bf16[512,128]{1,0:T(8,128)(2,1)S(1)}, u32[]{:S(2)}, u32[]{:S(2)}) collective-permute-start(bf16[512,128]{1,0:T(8,128)(2,1)} %v_hbm.1), channel_id=1, source_target_pairs={{0,2},{1,3},{2,4},{3,5},{4,6},{5,7},{6,8},{7,9},{8,10},{9,11},{10,... | collective-permute-start | bytes 393224 | tf_op jit(solution)/shard_map/ppermute | solution.py:25
  4.4 5.7 %own_shard.1 = (s32[4,8]{1,0:T(4,128)S(1)}, s32[4]{0:T(128)S(1)}, bf16[4096,128]{1,0:T(8,128)(2,1)S(1)}, bf16[4096,128]{1,0:T(8,128)(2,1)S(1)}, f32[4,1,1024]{2,...) custom-call(s32[1]{0:T(128)} %bitcast.position_ref, ...), custom_call_target="tpu_custom_call" | custom-call | flops 1 | bytes 1 | tf_op jit(solution)/shard_map/own_shard/pallas_call | solution.py:295
  10.1 0.0 collective-permute-done.refs_2_
  10.1 0.0 collective-permute-done.1.refs_3_
  10.1 0.1 collective-permute-start.4
  10.2 0.5 collective-permute-start.5
  10.7 0.1 collective-permute-start.6
  10.8 6.8 %collective-permute-start.2 = (bf16[512,128]{1,0:T(8,128)(2,1)S(1)}, bf16[512,128]{1,0:T(8,128)(2,1)S(1)}, u32[]{:S(2)}, u32[]{:S(2)}) collective-permute-start(bf16[512,128]{1,0:T(8,128)(2,1)S(1)} %collective-permute-done.refs_2_), channel_id=1, source_target_pairs={{0,2},{1,3},{2,4},{3,5},{4,6},{5,7},{6,8},{7,9},{8,10},{9,11},{10,... | collective-permute-start | bytes 393224 | tf_op jit(solution)/shard_map/ppermute | solution.py:25
  17.6 0.0 collective-permute-start.3
  17.6 0.0 collective-permute-done.5.refs_4_
  17.7 0.0 collective-permute-done.6.refs_5_
  17.7 0.0 collective-permute-done.4.refs_1_
  17.7 3.7 %near_shards.1 = (f32[4,128,1024]{2,1,0:T(8,128)S(1)}, bf16[256,128]{1,0:T(8,128)(2,1)S(1)}, bf16[256,128]{1,0:T(8,128)(2,1)S(1)}, bf16[256,128]{1,0:T(8,128)(2,...) custom-call(s32[1]{0:T(128)} %bitcast.position_ref, ...), custom_call_target="tpu_custom_call", output_to_operand_aliasing={{0}: (7, {})} | custom-call | flops 1 | bytes 1 | tf_op jit(solution)/shard_map/near_shards/pallas_call | solution.py:321
  21.4 0.1 collective-permute-start.13
  21.5 0.5 collective-permute-start.14
  22.0 0.1 collective-permute-start.15
  22.1 0.0 collective-permute-done.2.refs_1_
  22.1 0.4 collective-permute-start.16
  22.5 1.4 %collective-permute-done.3.refs_2_ = bf16[512,128]{1,0:T(8,128)(2,1)S(1)} collective-permute-done((bf16[512,128]{1,0:T(8,128)(2,1)S(1)}, bf16[512,128]{1,0:T(8,128)(2,1)S(1)}, u32[]{:S(2)}, u32[]{:S(2)}) %collective-permute-start.3) | collective-permute-done | bytes 131104 | tf_op jit(solution)/shard_map/ppermute | solution.py:25
  23.9 0.0 collective-permute-start.7
  23.9 0.0 collective-permute-done.13.refs_0_
  23.9 0.5 collective-permute-start.8
  24.4 0.0 collective-permute-done.14.refs_1_
  24.4 0.0 collective-permute-done.15.refs_2_
  24.4 0.0 collective-permute-done.16.refs_3_
  24.4 0.1 near_sum.1
  24.4 0.1 collective-permute-start.17
  24.5 0.7 %collective-permute-done.7.refs_3_ = bf16[512,128]{1,0:T(8,128)(2,1)S(1)} collective-permute-done((bf16[512,128]{1,0:T(8,128)(2,1)S(1)}, bf16[512,128]{1,0:T(8,128)(2,1)S(1)}, u32[]{:S(2)}, u32[]{:S(2)}) %collective-permute-start.7) | collective-permute-done | bytes 131104 | tf_op jit(solution)/shard_map/ppermute | solution.py:30
  25.2 0.2 collective-permute-done.8.refs_4_
  25.4 4.5 %far_shards.1 = (f32[4,128,1024]{2,1,0:T(8,128)S(1)}, bf16[512,128]{1,0:T(8,128)(2,1)S(1)}, bf16[512,128]{1,0:T(8,128)(2,1)S(1)}, bf16[1024,128]{1,0:T(8,128)(2,1)S(1)}) custom-call(s32[1]{0:T(128)} %bitcast.position_ref, s32[4,8]{1,0:T(4,128)S(1)} %get-tuple-element.38.list_ref, s32[4]{0:T(128)S(1)} %get-tuple-element.39.live_ref, ...), custom_call_target="tpu_custom_call", output_to_operand_aliasing={{0}: (7, {})} | custom-call | flops 1 | bytes 1 | tf_op jit(solution)/shard_map/far_shards/pallas_call | solution.py:321
  29.9 0.1 collective-permute-start.10
  30.0 0.5 collective-permute-start.9
  30.5 0.3 collective-permute-start.18
  30.8 0.5 collective-permute-done.10.refs_1_
  31.3 0.3 collective-permute-done.9.refs_0_
  31.7 0.1 far_sum.1
  31.7 0.1 collective-permute-start.11
  31.8 0.1 collective-permute-start.12
  31.9 9.8 %collective-permute-done.17 = bf16[1408,128]{1,0:T(8,128)(2,1)S(1)} collective-permute-done((bf16[1408,128]{1,0:T(8,128)(2,1)S(1)}, bf16[1408,128]{1,0:T(8,128)(2,1)S(1)}, u32[]{:S(2)}, u32[]{:S(2)}) %collective-permute-start.17) | collective-permute-done | bytes 360480 | tf_op jit(solution)/shard_map/ppermute | solution.py:25
  41.7 1.8 %query_grad.1 = bf16[4096,128]{1,0:T(8,128)(2,1)} custom-call(f32[4,128,1024]{2,1,0:T(8,128)S(1)} %get-tuple-element.65.dq_ref), custom_call_target="tpu_custom_call" | custom-call | flops 1 | bytes 1 | tf_op jit(solution)/shard_map/query_grad/pallas_call | solution.py:349
  43.5 8.1 %collective-permute-done.11 = bf16[512,128]{1,0:T(8,128)(2,1)S(1)} collective-permute-done((bf16[512,128]{1,0:T(8,128)(2,1)S(1)}, bf16[512,128]{1,0:T(8,128)(2,1)S(1)}, u32[]{:S(2)}, u32[]{:S(2)}) %collective-permute-start.11) | collective-permute-done | bytes 131104 | tf_op jit(solution)/shard_map/ppermute | solution.py:25
  51.6 1.9 %collective-permute-done.12 = bf16[512,128]{1,0:T(8,128)(2,1)S(1)} collective-permute-done((bf16[512,128]{1,0:T(8,128)(2,1)S(1)}, bf16[512,128]{1,0:T(8,128)(2,1)S(1)}, u32[]{:S(2)}, u32[]{:S(2)}) %collective-permute-start.12) | collective-permute-done | bytes 131104 | tf_op jit(solution)/shard_map/ppermute | solution.py:25
  53.4 0.0 collective-permute-done.18
  53.4 0.1 convert_add_fusion
  53.5 0.8 %fusion.1 = (bf16[512,128]{1,0:T(8,128)(2,1)}, bf16[512,128]{1,0:T(8,128)(2,1)}) fusion(f32[512,128]{1,0:T(8,128)S(1)} %get-tuple-element.71, f32[1024,128]{1,0:T(8,128)S(1)} %convert_add_fusion, bf16[512,128]{1,0:T(8,128)(2,1)S(1)} %collective-permute-done.12, bf16[512,128]{1,0:T(8,128)(2,1)S(1)} %collective-permute-done.11, f32[512,128]{1,0:T(8,128)S(1)} %get-tuple-element.67), kind=kLoop, calls=%fused_computation.3 | loop fusion | flops 524288 | bytes 1572864 | tf_op jit(solution)/shard_map/convert_element_type | solution.py:380
Async XLA Ops:
  0.6 9.5 %collective-permute-start = (bf16[512,128]{1,0:T(8,128)(2,1)}, bf16[512,128]{1,0:T(8,128)(2,1)S(1)}, u32[]{:S(2)}, u32[]{:S(2)}) collective-permute-start(bf16[512,128]{1,0:T(8,128)(2,1)} %k_hbm.1), channel_id=1, source_target_pairs={{0,2},{1,3},{2,4},{3,5},{4,6},{5,7},{6,8},{7,9},{8,10},{9,11},{10,... | collective-permute-start | bytes 393224 | tf_op jit(solution)/shard_map/ppermute | solution.py:25
  3.4 6.7 %collective-permute-start.1 = (bf16[512,128]{1,0:T(8,128)(2,1)}, bf16[512,128]{1,0:T(8,128)(2,1)S(1)}, u32[]{:S(2)}, u32[]{:S(2)}) collective-permute-start(bf16[512,128]{1,0:T(8,128)(2,1)} %v_hbm.1), channel_id=1, source_target_pairs={{0,2},{1,3},{2,4},{3,5},{4,6},{5,7},{6,8},{7,9},{8,10},{9,11},{10,... | collective-permute-start | bytes 393224 | tf_op jit(solution)/shard_map/ppermute | solution.py:25
  10.1 7.5 %collective-permute-start.4 = (bf16[1024,128]{1,0:T(8,128)(2,1)S(1)}, bf16[1024,128]{1,0:T(8,128)(2,1)S(1)}, u32[]{:S(2)}, u32[]{:S(2)}) collective-permute-start(bf16[1024,128]{1,0:T(8,128)(2,1)S(1)} %get-tuple-element.49), channel_id=1, source_target_pairs={{0,1},{1,0},{2,3},{3,2},{4,5},{5,4},{6,7},{7,6},{8,9},{9,8},{10,11... | collective-permute-start | bytes 786440 | tf_op jit(solution)/shard_map/ppermute | solution.py:30
  10.2 7.4 %collective-permute-start.5 = (bf16[512,128]{1,0:T(8,128)(2,1)S(1)}, bf16[512,128]{1,0:T(8,128)(2,1)S(1)}, u32[]{:S(2)}, u32[]{:S(2)}) collective-permute-start(bf16[512,128]{1,0:T(8,128)(2,1)S(1)} %collective-permute-done.refs_2_), channel_id=1, source_target_pairs={{0,1},{1,0},{2,3},{3,2},{4,5},{5,4},{6,7},{7,6},{8,9},{9,8},{10,11... | collective-permute-start | bytes 393224 | tf_op jit(solution)/shard_map/ppermute | solution.py:30
  10.7 6.9 %collective-permute-start.6 = (bf16[512,128]{1,0:T(8,128)(2,1)S(1)}, bf16[512,128]{1,0:T(8,128)(2,1)S(1)}, u32[]{:S(2)}, u32[]{:S(2)}) collective-permute-start(bf16[512,128]{1,0:T(8,128)(2,1)S(1)} %collective-permute-done.1.refs_3_), channel_id=1, source_target_pairs={{0,1},{1,0},{2,3},{3,2},{4,5},{5,4},{6,7},{7,6},{8,9},{9,8},{10,11... | collective-permute-start | bytes 393224 | tf_op jit(solution)/shard_map/ppermute | solution.py:30
  10.8 11.2 %collective-permute-start.2 = (bf16[512,128]{1,0:T(8,128)(2,1)S(1)}, bf16[512,128]{1,0:T(8,128)(2,1)S(1)}, u32[]{:S(2)}, u32[]{:S(2)}) collective-permute-start(bf16[512,128]{1,0:T(8,128)(2,1)S(1)} %collective-permute-done.refs_2_), channel_id=1, source_target_pairs={{0,2},{1,3},{2,4},{3,5},{4,6},{5,7},{6,8},{7,9},{8,10},{9,11},{10,... | collective-permute-start | bytes 393224 | tf_op jit(solution)/shard_map/ppermute | solution.py:25
  17.6 6.2 %collective-permute-start.3 = (bf16[512,128]{1,0:T(8,128)(2,1)S(1)}, bf16[512,128]{1,0:T(8,128)(2,1)S(1)}, u32[]{:S(2)}, u32[]{:S(2)}) collective-permute-start(bf16[512,128]{1,0:T(8,128)(2,1)S(1)} %collective-permute-done.1.refs_3_), channel_id=1, source_target_pairs={{0,2},{1,3},{2,4},{3,5},{4,6},{5,7},{6,8},{7,9},{8,10},{9,11},{10,... | collective-permute-start | bytes 393224 | tf_op jit(solution)/shard_map/ppermute | solution.py:25
  21.4 2.5 %collective-permute-start.13 = (bf16[256,128]{1,0:T(8,128)(2,1)S(1)}, bf16[256,128]{1,0:T(8,128)(2,1)S(1)}, u32[]{:S(2)}, u32[]{:S(2)}) collective-permute-start(bf16[256,128]{1,0:T(8,128)(2,1)S(1)} %get-tuple-element.60), channel_id=1, source_target_pairs={{0,1},{1,0},{2,3},{3,2},{4,5},{5,4},{6,7},{7,6},{8,9},{9,8},{10,11... | collective-permute-start | bytes 196616 | tf_op jit(solution)/shard_map/ppermute | solution.py:30
  21.5 2.9 %collective-permute-start.14 = (bf16[256,128]{1,0:T(8,128)(2,1)S(1)}, bf16[256,128]{1,0:T(8,128)(2,1)S(1)}, u32[]{:S(2)}, u32[]{:S(2)}) collective-permute-start(bf16[256,128]{1,0:T(8,128)(2,1)S(1)} %get-tuple-element.61), channel_id=1, source_target_pairs={{0,1},{1,0},{2,3},{3,2},{4,5},{5,4},{6,7},{7,6},{8,9},{9,8},{10,11... | collective-permute-start | bytes 196616 | tf_op jit(solution)/shard_map/ppermute | solution.py:30
  22.0 2.4 %collective-permute-start.15 = (bf16[256,128]{1,0:T(8,128)(2,1)S(1)}, bf16[256,128]{1,0:T(8,128)(2,1)S(1)}, u32[]{:S(2)}, u32[]{:S(2)}) collective-permute-start(bf16[256,128]{1,0:T(8,128)(2,1)S(1)} %get-tuple-element.62), channel_id=1, source_target_pairs={{0,1},{1,0},{2,3},{3,2},{4,5},{5,4},{6,7},{7,6},{8,9},{9,8},{10,11... | collective-permute-start | bytes 196616 | tf_op jit(solution)/shard_map/ppermute | solution.py:30
  22.1 2.3 %collective-permute-start.16 = (bf16[256,128]{1,0:T(8,128)(2,1)S(1)}, bf16[256,128]{1,0:T(8,128)(2,1)S(1)}, u32[]{:S(2)}, u32[]{:S(2)}) collective-permute-start(bf16[256,128]{1,0:T(8,128)(2,1)S(1)} %get-tuple-element.63), channel_id=1, source_target_pairs={{0,1},{1,0},{2,3},{3,2},{4,5},{5,4},{6,7},{7,6},{8,9},{9,8},{10,11... | collective-permute-start | bytes 196616 | tf_op jit(solution)/shard_map/ppermute | solution.py:30
  23.9 1.3 %collective-permute-start.7 = (bf16[512,128]{1,0:T(8,128)(2,1)S(1)}, bf16[512,128]{1,0:T(8,128)(2,1)S(1)}, u32[]{:S(2)}, u32[]{:S(2)}) collective-permute-start(bf16[512,128]{1,0:T(8,128)(2,1)S(1)} %collective-permute-done.2.refs_1_), channel_id=1, source_target_pairs={{0,1},{1,0},{2,3},{3,2},{4,5},{5,4},{6,7},{7,6},{8,9},{9,8},{10,11... | collective-permute-start | bytes 393224 | tf_op jit(solution)/shard_map/ppermute | solution.py:30
  23.9 1.5 %collective-permute-start.8 = (bf16[512,128]{1,0:T(8,128)(2,1)S(1)}, bf16[512,128]{1,0:T(8,128)(2,1)S(1)}, u32[]{:S(2)}, u32[]{:S(2)}) collective-permute-start(bf16[512,128]{1,0:T(8,128)(2,1)S(1)} %collective-permute-done.3.refs_2_), channel_id=1, source_target_pairs={{0,1},{1,0},{2,3},{3,2},{4,5},{5,4},{6,7},{7,6},{8,9},{9,8},{10,11... | collective-permute-start | bytes 393224 | tf_op jit(solution)/shard_map/ppermute | solution.py:30
  24.4 17.2 %collective-permute-start.17 = (bf16[1408,128]{1,0:T(8,128)(2,1)S(1)}, bf16[1408,128]{1,0:T(8,128)(2,1)S(1)}, u32[]{:S(2)}, u32[]{:S(2)}) collective-permute-start(bf16[1408,128]{1,0:T(8,128)(2,1)S(1)} %near_sum.1), channel_id=1, source_target_pairs={{0,254},{1,255},{2,0},{3,1},{4,2},{5,3},{6,4},{7,5},{8,6},{9,7},{1... | collective-permute-start | bytes 1081352 | tf_op jit(solution)/shard_map/ppermute | solution.py:25
  29.9 1.4 %collective-permute-start.10 = (bf16[512,128]{1,0:T(8,128)(2,1)S(1)}, bf16[512,128]{1,0:T(8,128)(2,1)S(1)}, u32[]{:S(2)}, u32[]{:S(2)}) collective-permute-start(bf16[512,128]{1,0:T(8,128)(2,1)S(1)} %get-tuple-element.56), channel_id=1, source_target_pairs={{0,1},{1,0},{2,3},{3,2},{4,5},{5,4},{6,7},{7,6},{8,9},{9,8},{10,11... | collective-permute-start | bytes 393224 | tf_op jit(solution)/shard_map/ppermute | solution.py:30
  30.0 1.7 %collective-permute-start.9 = (bf16[512,128]{1,0:T(8,128)(2,1)S(1)}, bf16[512,128]{1,0:T(8,128)(2,1)S(1)}, u32[]{:S(2)}, u32[]{:S(2)}) collective-permute-start(bf16[512,128]{1,0:T(8,128)(2,1)S(1)} %get-tuple-element.55), channel_id=1, source_target_pairs={{0,1},{1,0},{2,3},{3,2},{4,5},{5,4},{6,7},{7,6},{8,9},{9,8},{10,11... | collective-permute-start | bytes 393224 | tf_op jit(solution)/shard_map/ppermute | solution.py:30
  30.5 22.9 %collective-permute-start.18 = (bf16[1024,128]{1,0:T(8,128)(2,1)S(1)}, bf16[1024,128]{1,0:T(8,128)(2,1)S(1)}, u32[]{:S(2)}, u32[]{:S(2)}) collective-permute-start(bf16[1024,128]{1,0:T(8,128)(2,1)S(1)} %get-tuple-element.68), channel_id=1, source_target_pairs={{0,1},{1,0},{2,3},{3,2},{4,5},{5,4},{6,7},{7,6},{8,9},{9,8},{10,11... | collective-permute-start | bytes 786440 | tf_op jit(solution)/shard_map/ppermute | solution.py:30
  31.7 19.8 %collective-permute-start.11 = (bf16[512,128]{1,0:T(8,128)(2,1)S(1)}, bf16[512,128]{1,0:T(8,128)(2,1)S(1)}, u32[]{:S(2)}, u32[]{:S(2)}) collective-permute-start(bf16[512,128]{1,0:T(8,128)(2,1)S(1)} %get-tuple-element.57), channel_id=1, source_target_pairs={{0,252},{1,253},{2,254},{3,255},{4,0},{5,1},{6,2},{7,3},{8,4},{9,5... | collective-permute-start | bytes 393224 | tf_op jit(solution)/shard_map/ppermute | solution.py:25
  31.8 21.6 %collective-permute-start.12 = (bf16[512,128]{1,0:T(8,128)(2,1)S(1)}, bf16[512,128]{1,0:T(8,128)(2,1)S(1)}, u32[]{:S(2)}, u32[]{:S(2)}) collective-permute-start(bf16[512,128]{1,0:T(8,128)(2,1)S(1)} %get-tuple-element.58), channel_id=1, source_target_pairs={{0,252},{1,253},{2,254},{3,255},{4,0},{5,1},{6,2},{7,3},{8,4},{9,5... | collective-permute-start | bytes 393224 | tf_op jit(solution)/shard_map/ppermute | solution.py:25
where the time goes:
time: 55.2 us; the launch traced here: 54.3 us
  waiting for transfers between devices  22.8 us (41%)
  Pallas kernels  15.8 us (29%)
  starting transfers between devices  14.1 us (26%)
  other arithmetic  0.83 us (2%)
  between operations  0.75 us (1%)
    ppermute x7, waiting for transfers between devices, ring_shift(): return lax.ppermute(block, AXES, route)  21.1 us
    ppermute x7, starting transfers between devices, ring_shift(): return lax.ppermute(block, AXES, route)  10.9 us
    pallas_call x2, Pallas kernels, shards_call(): pl.pallas_call(functools.partial(shards_kernel, scale=scale, parts=len(pa...  8.22 us
    pallas_call x1, Pallas kernels, own_call(): pl.pallas_call(functools.partial(own_kernel, scale=scale), in_specs=[smem...  5.66 us
    ppermute x12, starting transfers between devices, pair_swap(): return lax.ppermute(block, AXES, [(i, i ^ 1) for i in range(count)])  3.21 us
    pallas_call x1, Pallas kernels, finish_call(): pl.pallas_call(functools.partial(finish_kernel, scale=scale), grid=(local...  1.83 us
    ppermute x12, waiting for transfers between devices, pair_swap(): return lax.ppermute(block, AXES, [(i, i ^ 1) for i in range(count)])  1.7 us
  transfers between devices with their start and end apart: 19, of which 8 were waited for; matrix products, arithmetic and copies ran while one was open for 0% of the time, Pallas kernels for 29%

commit v1 on v0

--- a/solution.py
+++ b/solution.py
@@ -10,7 +10,7 @@
 BLOCK = 128
 CODE_BITS = 4
 CODES = 1 << CODE_BITS
-SPARE = 384
+SPARE = 16
 AXES = ("inner", "outer")
 LOG2E = 1.4426950408889634
 NT = (((1,), (1,)), ((), ()))
@@ -131,8 +131,8 @@
 
 
 def own_kernel(
-    position_ref, list_hbm, live_hbm, q_hbm, g_hbm, o_hbm, norm_hbm, k_hbm, v_hbm,
-    list_out, live_out, q_ref, g_ref, norm_ref, delta_ref, dq_ref, dk_ref, dv_ref, both_ref,
+    position_ref, list_hbm, live_hbm, q_hbm, g_hbm, o_hbm, norm_hbm, both_ref,
+    list_out, live_out, q_ref, g_ref, norm_ref, delta_ref, dq_ref, dk_ref, dv_ref,
     o_ref, raw_ref, list_ref, live_ref, items_ref, row_sems, sems, *, scale,
 ):
     local_blocks = list_ref.shape[0]
@@ -145,7 +145,7 @@
         pltpu.make_async_copy(source, target, sems.at[index])
         for index, (source, target) in enumerate(
             (
-                (norm_hbm, raw_ref), (k_hbm, k_ref), (v_hbm, v_ref), (list_hbm, list_ref),
+                (norm_hbm, raw_ref), (list_hbm, list_ref),
                 (live_hbm, live_ref), (list_hbm, list_out), (live_hbm, live_out),
             )
         )
@@ -250,6 +250,18 @@
         out_refs[0][span, :] = jnp.zeros((SPARE, straight_ref.shape[1]), BF16)
 
 
+def stack_kernel(k_hbm, v_hbm, out_ref, sems):
+    tokens = k_hbm.shape[0]
+    copies = [
+        pltpu.make_async_copy(source, out_ref.at[pl.ds(half * tokens, tokens), :], sems.at[half])
+        for half, source in enumerate((k_hbm, v_hbm))
+    ]
+    for copy in copies:
+        copy.start()
+    for copy in copies:
+        copy.wait()
+
+
 def finish_kernel(dq_ref, out_ref, *, scale):
     out_ref[...] = (dq_ref[0] * scale).T.astype(out_ref.dtype)
 
@@ -294,15 +306,15 @@
     def own_call():
         outs = pl.pallas_call(
             functools.partial(own_kernel, scale=scale),
-            in_specs=[smem] + [anywhere] * 8,
-            out_specs=[vmem] * 10,
+            in_specs=[smem] + [anywhere] * 6 + [vmem],
+            out_specs=[vmem] * 9,
             out_shape=[pltpu.VMEM(block_list.shape, jnp.int32)]
             + [pltpu.VMEM(block_live.shape, jnp.int32)]
-            + [rows_shape] * 2 + [line_shape] * 2 + [dq_shape] + [wide_shape] * 2 + [stacked(2)],
+            + [rows_shape] * 2 + [line_shape] * 2 + [dq_shape] + [wide_shape] * 2,
             scratch_shapes=[
                 pltpu.VMEM(all_rows, BF16), pltpu.VMEM((heads, local_tokens), F32),
                 pltpu.SMEM(block_list.shape, jnp.int32), pltpu.SMEM(block_live.shape, jnp.int32),
-                items, pltpu.SemaphoreType.DMA((3, local_blocks)), pltpu.SemaphoreType.DMA((7,)),
+                items, pltpu.SemaphoreType.DMA((3, local_blocks)), pltpu.SemaphoreType.DMA((5,)),
             ],
             compiler_params=params,
             cost_estimate=cost(1),
@@ -311,7 +323,7 @@
             device, in_hbm(block_list), in_hbm(block_live),
             in_hbm(queries.reshape(all_rows)), in_hbm(out_grad.reshape(all_rows)),
             in_hbm(forward_out.reshape(all_rows)), in_hbm(log_norm.T),
-            in_hbm(key_tokens), in_hbm(value_tokens),
+            in_vmem(kv),
         )
         return [in_vmem(x) for x in outs[:7]] + list(outs[7:])
 
@@ -323,9 +335,9 @@
                 shards_kernel, scale=scale, parts=len(parts), shards=shards, place_of=place_of
             ),
             in_specs=[smem] * 3 + [vmem] * (5 + len(parts)),
-            out_specs=[vmem] * (shards + (4 if shards == 3 else 2)),
+            out_specs=[vmem] * (shards + 2),
             out_shape=[dq_shape]
-            + ([quarter] * 4 if shards == 3 else [stacked(1)] * 2)
+            + [stacked(1)] * 2
             + [stacked(2)] * (shards - 1),
             scratch_shapes=[narrow, narrow, wide, wide, items],
             input_output_aliases={7: 0},
@@ -344,6 +356,18 @@
             cost_estimate=cost(1),
             name=name,
         )(*map(in_vmem, (straight, *crossed)))
+
+    def stack_call():
+        return pl.pallas_call(
+            stack_kernel,
+            in_specs=[anywhere] * 2,
+            out_specs=vmem,
+            out_shape=stacked(2),
+            scratch_shapes=[pltpu.SemaphoreType.DMA((2,))],
+            compiler_params=params,
+            cost_estimate=cost(1),
+            name="stack",
+        )(in_hbm(key_tokens), in_hbm(value_tokens))
 
     def finish_call(dq):
         return pl.pallas_call(
@@ -358,18 +382,17 @@
         )(in_vmem(dq))
 
     k2, v2 = ring_shift(key_tokens, 2), ring_shift(value_tokens, 2)
-    listed, live, q, g, norm, delta, dq, dk0, dv0, kv = own_call()
-    k2, v2, kv, dq = lax.optimization_barrier((k2, v2, kv, dq))
-    k4, v4 = ring_shift(k2, 2), ring_shift(v2, 2)
+    kv = stack_call()
+    kv4 = ring_shift(kv, 4)
+    listed, live, q, g, norm, delta, dq, dk0, dv0 = own_call()
+    k2, v2, dq = lax.optimization_barrier((k2, v2, dq))
     dq, *crossed, near, other = shards_call(
         dq, (pair_swap(kv), k2, v2, pair_swap(k2), pair_swap(v2)), 3, near_place, "near_shards"
     )
     (near,) = add_call(near, [pair_swap(x) for x in crossed], [spare_shape], "near_sum")
     near = ring_shift(near, -2)
-    k4, v4, dq = lax.optimization_barrier((k4, v4, dq))
-    dq, *crossed, far = shards_call(
-        dq, (k4, v4, pair_swap(k4), pair_swap(v4)), 2, far_place, "far_shards"
-    )
+    kv4, dq = lax.optimization_barrier((kv4, dq))
+    dq, *crossed, far = shards_call(dq, (kv4, pair_swap(kv4)), 2, far_place, "far_shards")
     far = add_call(far, [pair_swap(x) for x in crossed], [stacked(1)] * 2, "far_sum")
     far_k, far_v = (ring_shift(part, -4) for part in far)
     near, dq = lax.optimization_barrier((near, dq))

time: 55.2 us -> 51.4 us (0.931)
  the two profiles are of different devices: /device:TPU:126 before, /device:TPU:32 now
where the time goes in v1:
time: 51.4 us; the launch traced here: 50.4 us
  starting transfers between devices  19.4 us (38%)
  waiting for transfers between devices  16.1 us (31%)
  Pallas kernels  13.3 us (26%)
  other arithmetic  0.86 us (2%)
  between operations  0.71 us (1%)
    ppermute x6, starting transfers between devices, ring_shift(): return lax.ppermute(block, AXES, route)  14.3 us
    ppermute x6, waiting for transfers between devices, ring_shift(): return lax.ppermute(block, AXES, route)  13.3 us
    pallas_call x2, Pallas kernels, shards_call(): pl.pallas_call(functools.partial(shards_kernel, scale=scale, parts=len(pa...  5.31 us
    ppermute x9, starting transfers between devices, pair_swap(): return lax.ppermute(block, AXES, [(i, i ^ 1) for i in range(count)])  5.08 us
    pallas_call x1, Pallas kernels, own_call(): pl.pallas_call(functools.partial(own_kernel, scale=scale), in_specs=[smem...  4.97 us
    ppermute x9, waiting for transfers between devices, pair_swap(): return lax.ppermute(block, AXES, [(i, i ^ 1) for i in range(count)])  2.87 us
    pallas_call x1, Pallas kernels, finish_call(): pl.pallas_call(functools.partial(finish_kernel, scale=scale), grid=(local...  1.83 us
  transfers between devices with their start and end apart: 15, of which 9 were waited for; matrix products, arithmetic and copies ran while one was open for 0% of the time, Pallas kernels for 26%

profile of v1, /device:TPU:32, one launch (start us, length us, event | category | flops | bytes accessed | tf_op | source)
XLA Modules:
  0.0 50.4 jit_solution(15286210119742746846)
XLA Ops:
  0.6 2.0 %collective-permute-start.1 = (bf16[512,128]{1,0:T(8,128)(2,1)}, bf16[512,128]{1,0:T(8,128)(2,1)S(1)}, u32[]{:S(2)}, u32[]{:S(2)}) collective-permute-start(bf16[512,128]{1,0:T(8,128)(2,1)} %k_hbm.1), channel_id=1, source_target_pairs={{0,2},{1,3},{2,4},{3,5},{4,6},{5,7},{6,8},{7,9},{8,10},{9,11},{10,... | collective-permute-start | bytes 393224 | tf_op jit(solution)/shard_map/ppermute | solution.py:25
  2.6 1.9 %collective-permute-start.2 = (bf16[512,128]{1,0:T(8,128)(2,1)}, bf16[512,128]{1,0:T(8,128)(2,1)S(1)}, u32[]{:S(2)}, u32[]{:S(2)}) collective-permute-start(bf16[512,128]{1,0:T(8,128)(2,1)} %v_hbm.1), channel_id=1, source_target_pairs={{0,2},{1,3},{2,4},{3,5},{4,6},{5,7},{6,8},{7,9},{8,10},{9,11},{10,... | collective-permute-start | bytes 393224 | tf_op jit(solution)/shard_map/ppermute | solution.py:25
  4.5 1.0 %stack.1.both_ref = bf16[1024,128]{1,0:T(8,128)(2,1)S(1)} custom-call(bf16[512,128]{1,0:T(8,128)(2,1)} %k_hbm.1, bf16[512,128]{1,0:T(8,128)(2,1)} %v_hbm.1), custom_call_target="tpu_custom_call" | custom-call | flops 1 | bytes 1 | tf_op jit(solution)/shard_map/stack/pallas_call | solution.py:361
  5.5 0.1 collective-permute-start.3
  5.6 1.6 %collective-permute-start = (bf16[1024,128]{1,0:T(8,128)(2,1)S(1)}, bf16[1024,128]{1,0:T(8,128)(2,1)S(1)}, u32[]{:S(2)}, u32[]{:S(2)}) collective-permute-start(bf16[1024,128]{1,0:T(8,128)(2,1)S(1)} %stack.1.both_ref), channel_id=1, source_target_pairs={{0,4},{1,5},{2,6},{3,7},{4,8},{5,9},{6,10},{7,11},{8,12},{9,13},{1... | collective-permute-start | bytes 786440 | tf_op jit(solution)/shard_map/ppermute | solution.py:25
  7.3 5.0 %own_shard.1 = (s32[4,8]{1,0:T(4,128)S(1)}, s32[4]{0:T(128)S(1)}, bf16[4096,128]{1,0:T(8,128)(2,1)S(1)}, bf16[4096,128]{1,0:T(8,128)(2,1)S(1)}, f32[4,1,1024]{2,...) custom-call(s32[1]{0:T(128)} %bitcast.position_ref, ...), custom_call_target="tpu_custom_call" | custom-call | flops 1 | bytes 1 | tf_op jit(solution)/shard_map/own_shard/pallas_call | solution.py:307
  12.3 0.0 collective-permute-done.1.refs_2_
  12.3 2.5 %collective-permute-done.2.refs_3_ = bf16[512,128]{1,0:T(8,128)(2,1)S(1)} collective-permute-done((bf16[512,128]{1,0:T(8,128)(2,1)}, bf16[512,128]{1,0:T(8,128)(2,1)S(1)}, u32[]{:S(2)}, u32[]{:S(2)}) %collective-permute-start.2) | collective-permute-done | bytes 131104 | tf_op jit(solution)/shard_map/ppermute | solution.py:25
  14.8 0.0 collective-permute-start.4
  14.8 0.5 %collective-permute-start.5 = (bf16[512,128]{1,0:T(8,128)(2,1)S(1)}, bf16[512,128]{1,0:T(8,128)(2,1)S(1)}, u32[]{:S(2)}, u32[]{:S(2)}) collective-permute-start(bf16[512,128]{1,0:T(8,128)(2,1)S(1)} %collective-permute-done.2.refs_3_), channel_id=1, source_target_pairs={{0,1},{1,0},{2,3},{3,2},{4,5},{5,4},{6,7},{7,6},{8,9},{9,8},{10,11... | collective-permute-start | bytes 393224 | tf_op jit(solution)/shard_map/ppermute | solution.py:30
  15.3 0.0 collective-permute-done.3.refs_1_
  15.3 0.8 %collective-permute-done.4.refs_4_ = bf16[512,128]{1,0:T(8,128)(2,1)S(1)} collective-permute-done((bf16[512,128]{1,0:T(8,128)(2,1)S(1)}, bf16[512,128]{1,0:T(8,128)(2,1)S(1)}, u32[]{:S(2)}, u32[]{:S(2)}) %collective-permute-start.4) | collective-permute-done | bytes 131104 | tf_op jit(solution)/shard_map/ppermute | solution.py:30
  16.2 0.2 collective-permute-done.5.refs_5_
  16.4 4.4 %near_shards.1 = (f32[4,128,1024]{2,1,0:T(8,128)S(1)}, bf16[512,128]{1,0:T(8,128)(2,1)S(1)}, bf16[512,128]{1,0:T(8,128)(2,1)S(1)}, bf16[1024,128]{1,0:T(8,128)(2,1)S(1)}, bf16[1024,128]{1,0:T(8,128)(2,1)S(1)}) custom-call(s32[1]{0:T(128)} %bitcast.position_ref, s32[4,8]{1,0:T(4,128)S(1)} %get-tuple-element.33.list_ref, ...), custom_call_target="tpu_custom_call", output_to_operand_aliasing={{0}: (7, {})} | custom-call | flops 1 | bytes 1 | tf_op jit(solution)/shard_map/near_shards/pallas_call | solution.py:333
  20.7 3.2 %collective-permute-start.11 = (bf16[512,128]{1,0:T(8,128)(2,1)S(1)}, bf16[512,128]{1,0:T(8,128)(2,1)S(1)}, u32[]{:S(2)}, u32[]{:S(2)}) collective-permute-start(bf16[512,128]{1,0:T(8,128)(2,1)S(1)} %get-tuple-element.52), channel_id=1, source_target_pairs={{0,1},{1,0},{2,3},{3,2},{4,5},{5,4},{6,7},{7,6},{8,9},{9,8},{10,11... | collective-permute-start | bytes 393224 | tf_op jit(solution)/shard_map/ppermute | solution.py:30
  23.9 0.1 collective-permute-start.12
  24.0 4.5 %collective-permute-done.refs_1_ = bf16[1024,128]{1,0:T(8,128)(2,1)S(1)} collective-permute-done((bf16[1024,128]{1,0:T(8,128)(2,1)S(1)}, bf16[1024,128]{1,0:T(8,128)(2,1)S(1)}, u32[]{:S(2)}, u32[]{:S(2)}) %collective-permute-start) | collective-permute-done | bytes 262176 | tf_op jit(solution)/shard_map/ppermute | solution.py:25
  28.5 0.0 collective-permute-start.6
  28.5 0.0 collective-permute-done.11.refs_0_
  28.5 0.0 collective-permute-done.12.refs_1_
  28.5 0.1 near_sum.1
  28.6 0.1 collective-permute-start.13
  28.7 0.6 %collective-permute-start.14 = (bf16[1024,128]{1,0:T(8,128)(2,1)S(1)}, bf16[1024,128]{1,0:T(8,128)(2,1)S(1)}, u32[]{:S(2)}, u32[]{:S(2)}) collective-permute-start(bf16[1024,128]{1,0:T(8,128)(2,1)S(1)} %get-tuple-element.58), channel_id=1, source_target_pairs={{0,1},{1,0},{2,3},{3,2},{4,5},{5,4},{6,7},{7,6},{8,9},{9,8},{10,11... | collective-permute-start | bytes 786440 | tf_op jit(solution)/shard_map/ppermute | solution.py:30
  29.3 0.8 %collective-permute-done.6.refs_2_ = bf16[1024,128]{1,0:T(8,128)(2,1)S(1)} collective-permute-done((bf16[1024,128]{1,0:T(8,128)(2,1)S(1)}, bf16[1024,128]{1,0:T(8,128)(2,1)S(1)}, u32[]{:S(2)}, u32[]{:S(2)}) %collective-permute-start.6) | collective-permute-done | bytes 262176 | tf_op jit(solution)/shard_map/ppermute | solution.py:30
  30.0 0.9 %far_shards.1 = (f32[4,128,1024]{2,1,0:T(8,128)S(1)}, bf16[512,128]{1,0:T(8,128)(2,1)S(1)}, bf16[512,128]{1,0:T(8,128)(2,1)S(1)}, bf16[1024,128]{1,0:T(8,128)(2,1)S(1)}) custom-call(s32[1]{0:T(128)} %bitcast.position_ref, s32[4,8]{1,0:T(4,128)S(1)} %get-tuple-element.33.list_ref, s32[4]{0:T(128)S(1)} %get-tuple-element.34.live_ref, ...), custom_call_target="tpu_custom_call", output_to_operand_aliasing={{0}: (7, {})} | custom-call | flops 1 | bytes 1 | tf_op jit(solution)/shard_map/far_shards/pallas_call | solution.py:333
  31.0 0.3 collective-permute-start.7
  31.3 0.3 collective-permute-start.8
  31.6 0.8 %collective-permute-done.7.refs_0_ = bf16[512,128]{1,0:T(8,128)(2,1)S(1)} collective-permute-done((bf16[512,128]{1,0:T(8,128)(2,1)S(1)}, bf16[512,128]{1,0:T(8,128)(2,1)S(1)}, u32[]{:S(2)}, u32[]{:S(2)}) %collective-permute-start.7) | collective-permute-done | bytes 131104 | tf_op jit(solution)/shard_map/ppermute | solution.py:30
  32.4 0.2 collective-permute-done.8.refs_1_
  32.7 0.1 far_sum.1
  32.7 5.2 %collective-permute-start.9 = (bf16[512,128]{1,0:T(8,128)(2,1)S(1)}, bf16[512,128]{1,0:T(8,128)(2,1)S(1)}, u32[]{:S(2)}, u32[]{:S(2)}) collective-permute-start(bf16[512,128]{1,0:T(8,128)(2,1)S(1)} %get-tuple-element.49), channel_id=1, source_target_pairs={{0,252},{1,253},{2,254},{3,255},{4,0},{5,1},{6,2},{7,3},{8,4},{9,5... | collective-permute-start | bytes 393224 | tf_op jit(solution)/shard_map/ppermute | solution.py:25
  37.9 3.5 %collective-permute-start.10 = (bf16[512,128]{1,0:T(8,128)(2,1)S(1)}, bf16[512,128]{1,0:T(8,128)(2,1)S(1)}, u32[]{:S(2)}, u32[]{:S(2)}) collective-permute-start(bf16[512,128]{1,0:T(8,128)(2,1)S(1)} %get-tuple-element.50), channel_id=1, source_target_pairs={{0,252},{1,253},{2,254},{3,255},{4,0},{5,1},{6,2},{7,3},{8,4},{9,5... | collective-permute-start | bytes 393224 | tf_op jit(solution)/shard_map/ppermute | solution.py:25
  41.4 0.0 collective-permute-done.13
  41.4 1.8 %query_grad.1 = bf16[4096,128]{1,0:T(8,128)(2,1)} custom-call(f32[4,128,1024]{2,1,0:T(8,128)S(1)} %get-tuple-element.55.dq_ref), custom_call_target="tpu_custom_call" | custom-call | flops 1 | bytes 1 | tf_op jit(solution)/shard_map/query_grad/pallas_call | solution.py:373
  43.3 0.0 collective-permute-done.14
  43.3 0.1 convert_add_fusion
  43.3 3.9 %collective-permute-done.9 = bf16[512,128]{1,0:T(8,128)(2,1)S(1)} collective-permute-done((bf16[512,128]{1,0:T(8,128)(2,1)S(1)}, bf16[512,128]{1,0:T(8,128)(2,1)S(1)}, u32[]{:S(2)}, u32[]{:S(2)}) %collective-permute-start.9) | collective-permute-done | bytes 131104 | tf_op jit(solution)/shard_map/ppermute | solution.py:25
  47.2 2.3 %collective-permute-done.10 = bf16[512,128]{1,0:T(8,128)(2,1)S(1)} collective-permute-done((bf16[512,128]{1,0:T(8,128)(2,1)S(1)}, bf16[512,128]{1,0:T(8,128)(2,1)S(1)}, u32[]{:S(2)}, u32[]{:S(2)}) %collective-permute-start.10) | collective-permute-done | bytes 131104 | tf_op jit(solution)/shard_map/ppermute | solution.py:25
  49.6 0.8 %fusion.1 = (bf16[512,128]{1,0:T(8,128)(2,1)}, bf16[512,128]{1,0:T(8,128)(2,1)}) fusion(f32[512,128]{1,0:T(8,128)S(1)} %get-tuple-element.61, f32[1024,128]{1,0:T(8,128)S(1)} %convert_add_fusion, bf16[512,128]{1,0:T(8,128)(2,1)S(1)} %collective-permute-done.10, bf16[512,128]{1,0:T(8,128)(2,1)S(1)} %collective-permute-done.9, f32[512,128]{1,0:T(8,128)S(1)} %get-tuple-element.57), kind=kLoop, calls=%fused_computation.3 | loop fusion | flops 524288 | bytes 1572864 | tf_op jit(solution)/shard_map/convert_element_type | solution.py:403
Async XLA Ops:
  0.6 11.6 %collective-permute-start.1 = (bf16[512,128]{1,0:T(8,128)(2,1)}, bf16[512,128]{1,0:T(8,128)(2,1)S(1)}, u32[]{:S(2)}, u32[]{:S(2)}) collective-permute-start(bf16[512,128]{1,0:T(8,128)(2,1)} %k_hbm.1), channel_id=1, source_target_pairs={{0,2},{1,3},{2,4},{3,5},{4,6},{5,7},{6,8},{7,9},{8,10},{9,11},{10,... | collective-permute-start | bytes 393224 | tf_op jit(solution)/shard_map/ppermute | solution.py:25
  2.6 12.2 %collective-permute-start.2 = (bf16[512,128]{1,0:T(8,128)(2,1)}, bf16[512,128]{1,0:T(8,128)(2,1)S(1)}, u32[]{:S(2)}, u32[]{:S(2)}) collective-permute-start(bf16[512,128]{1,0:T(8,128)(2,1)} %v_hbm.1), channel_id=1, source_target_pairs={{0,2},{1,3},{2,4},{3,5},{4,6},{5,7},{6,8},{7,9},{8,10},{9,11},{10,... | collective-permute-start | bytes 393224 | tf_op jit(solution)/shard_map/ppermute | solution.py:25
  5.5 9.8 %collective-permute-start.3 = (bf16[1024,128]{1,0:T(8,128)(2,1)S(1)}, bf16[1024,128]{1,0:T(8,128)(2,1)S(1)}, u32[]{:S(2)}, u32[]{:S(2)}) collective-permute-start(bf16[1024,128]{1,0:T(8,128)(2,1)S(1)} %stack.1.both_ref), channel_id=1, source_target_pairs={{0,1},{1,0},{2,3},{3,2},{4,5},{5,4},{6,7},{7,6},{8,9},{9,8},{10,11... | collective-permute-start | bytes 786440 | tf_op jit(solution)/shard_map/ppermute | solution.py:30
  5.6 22.9 %collective-permute-start = (bf16[1024,128]{1,0:T(8,128)(2,1)S(1)}, bf16[1024,128]{1,0:T(8,128)(2,1)S(1)}, u32[]{:S(2)}, u32[]{:S(2)}) collective-permute-start(bf16[1024,128]{1,0:T(8,128)(2,1)S(1)} %stack.1.both_ref), channel_id=1, source_target_pairs={{0,4},{1,5},{2,6},{3,7},{4,8},{5,9},{6,10},{7,11},{8,12},{9,13},{1... | collective-permute-start | bytes 786440 | tf_op jit(solution)/shard_map/ppermute | solution.py:25
  14.8 1.3 %collective-permute-start.4 = (bf16[512,128]{1,0:T(8,128)(2,1)S(1)}, bf16[512,128]{1,0:T(8,128)(2,1)S(1)}, u32[]{:S(2)}, u32[]{:S(2)}) collective-permute-start(bf16[512,128]{1,0:T(8,128)(2,1)S(1)} %collective-permute-done.1.refs_2_), channel_id=1, source_target_pairs={{0,1},{1,0},{2,3},{3,2},{4,5},{5,4},{6,7},{7,6},{8,9},{9,8},{10,11... | collective-permute-start | bytes 393224 | tf_op jit(solution)/shard_map/ppermute | solution.py:30
  14.8 1.5 %collective-permute-start.5 = (bf16[512,128]{1,0:T(8,128)(2,1)S(1)}, bf16[512,128]{1,0:T(8,128)(2,1)S(1)}, u32[]{:S(2)}, u32[]{:S(2)}) collective-permute-start(bf16[512,128]{1,0:T(8,128)(2,1)S(1)} %collective-permute-done.2.refs_3_), channel_id=1, source_target_pairs={{0,1},{1,0},{2,3},{3,2},{4,5},{5,4},{6,7},{7,6},{8,9},{9,8},{10,11... | collective-permute-start | bytes 393224 | tf_op jit(solution)/shard_map/ppermute | solution.py:30
  20.7 7.8 %collective-permute-start.11 = (bf16[512,128]{1,0:T(8,128)(2,1)S(1)}, bf16[512,128]{1,0:T(8,128)(2,1)S(1)}, u32[]{:S(2)}, u32[]{:S(2)}) collective-permute-start(bf16[512,128]{1,0:T(8,128)(2,1)S(1)} %get-tuple-element.52), channel_id=1, source_target_pairs={{0,1},{1,0},{2,3},{3,2},{4,5},{5,4},{6,7},{7,6},{8,9},{9,8},{10,11... | collective-permute-start | bytes 393224 | tf_op jit(solution)/shard_map/ppermute | solution.py:30
  23.9 4.6 %collective-permute-start.12 = (bf16[512,128]{1,0:T(8,128)(2,1)S(1)}, bf16[512,128]{1,0:T(8,128)(2,1)S(1)}, u32[]{:S(2)}, u32[]{:S(2)}) collective-permute-start(bf16[512,128]{1,0:T(8,128)(2,1)S(1)} %get-tuple-element.53), channel_id=1, source_target_pairs={{0,1},{1,0},{2,3},{3,2},{4,5},{5,4},{6,7},{7,6},{8,9},{9,8},{10,11... | collective-permute-start | bytes 393224 | tf_op jit(solution)/shard_map/ppermute | solution.py:30
  28.5 1.5 %collective-permute-start.6 = (bf16[1024,128]{1,0:T(8,128)(2,1)S(1)}, bf16[1024,128]{1,0:T(8,128)(2,1)S(1)}, u32[]{:S(2)}, u32[]{:S(2)}) collective-permute-start(bf16[1024,128]{1,0:T(8,128)(2,1)S(1)} %collective-permute-done.refs_1_), channel_id=1, source_target_pairs={{0,1},{1,0},{2,3},{3,2},{4,5},{5,4},{6,7},{7,6},{8,9},{9,8},{10,11... | collective-permute-start | bytes 786440 | tf_op jit(solution)/shard_map/ppermute | solution.py:30
  28.6 12.8 %collective-permute-start.13 = (bf16[1040,128]{1,0:T(8,128)(2,1)S(1)}, bf16[1040,128]{1,0:T(8,128)(2,1)S(1)}, u32[]{:S(2)}, u32[]{:S(2)}) collective-permute-start(bf16[1040,128]{1,0:T(8,128)(2,1)S(1)} %near_sum.1), channel_id=1, source_target_pairs={{0,254},{1,255},{2,0},{3,1},{4,2},{5,3},{6,4},{7,5},{8,6},{9,7},{1... | collective-permute-start | bytes 798728 | tf_op jit(solution)/shard_map/ppermute | solution.py:25
  28.7 14.6 %collective-permute-start.14 = (bf16[1024,128]{1,0:T(8,128)(2,1)S(1)}, bf16[1024,128]{1,0:T(8,128)(2,1)S(1)}, u32[]{:S(2)}, u32[]{:S(2)}) collective-permute-start(bf16[1024,128]{1,0:T(8,128)(2,1)S(1)} %get-tuple-element.58), channel_id=1, source_target_pairs={{0,1},{1,0},{2,3},{3,2},{4,5},{5,4},{6,7},{7,6},{8,9},{9,8},{10,11... | collective-permute-start | bytes 786440 | tf_op jit(solution)/shard_map/ppermute | solution.py:30
  31.0 1.4 %collective-permute-start.7 = (bf16[512,128]{1,0:T(8,128)(2,1)S(1)}, bf16[512,128]{1,0:T(8,128)(2,1)S(1)}, u32[]{:S(2)}, u32[]{:S(2)}) collective-permute-start(bf16[512,128]{1,0:T(8,128)(2,1)S(1)} %get-tuple-element.47), channel_id=1, source_target_pairs={{0,1},{1,0},{2,3},{3,2},{4,5},{5,4},{6,7},{7,6},{8,9},{9,8},{10,11... | collective-permute-start | bytes 393224 | tf_op jit(solution)/shard_map/ppermute | solution.py:30
  31.3 1.3 %collective-permute-start.8 = (bf16[512,128]{1,0:T(8,128)(2,1)S(1)}, bf16[512,128]{1,0:T(8,128)(2,1)S(1)}, u32[]{:S(2)}, u32[]{:S(2)}) collective-permute-start(bf16[512,128]{1,0:T(8,128)(2,1)S(1)} %get-tuple-element.48), channel_id=1, source_target_pairs={{0,1},{1,0},{2,3},{3,2},{4,5},{5,4},{6,7},{7,6},{8,9},{9,8},{10,11... | collective-permute-start | bytes 393224 | tf_op jit(solution)/shard_map/ppermute | solution.py:30
  32.7 14.5 %collective-permute-start.9 = (bf16[512,128]{1,0:T(8,128)(2,1)S(1)}, bf16[512,128]{1,0:T(8,128)(2,1)S(1)}, u32[]{:S(2)}, u32[]{:S(2)}) collective-permute-start(bf16[512,128]{1,0:T(8,128)(2,1)S(1)} %get-tuple-element.49), channel_id=1, source_target_pairs={{0,252},{1,253},{2,254},{3,255},{4,0},{5,1},{6,2},{7,3},{8,4},{9,5... | collective-permute-start | bytes 393224 | tf_op jit(solution)/shard_map/ppermute | solution.py:25
  37.9 11.7 %collective-permute-start.10 = (bf16[512,128]{1,0:T(8,128)(2,1)S(1)}, bf16[512,128]{1,0:T(8,128)(2,1)S(1)}, u32[]{:S(2)}, u32[]{:S(2)}) collective-permute-start(bf16[512,128]{1,0:T(8,128)(2,1)S(1)} %get-tuple-element.50), channel_id=1, source_target_pairs={{0,252},{1,253},{2,254},{3,255},{4,0},{5,1},{6,2},{7,3},{8,4},{9,5... | collective-permute-start | bytes 393224 | tf_op jit(solution)/shard_map/ppermute | solution.py:25

commit v2 on v1

--- a/solution.py
+++ b/solution.py
@@ -224,12 +224,16 @@
         counts, items_ref, k_all, v_all, q_ref, g_ref, norm_ref,
         delta_ref, dq_ref, dk_acc, dv_acc, scale,
     )
-    pieces = len(outs) - shards + 1
+    pieces = 2
     size = 2 * tokens // pieces
     for index in range(pieces // 2):
         span = pl.ds((shards - 1) * tokens + index * size, size)
         outs[index][...] = (dk_acc[span, :] * scale).astype(BF16)
         outs[pieces // 2 + index][...] = dv_acc[span, :].astype(BF16)
+    if shards == 2:
+        outs[2][...] = (dk_acc[pl.ds(0, tokens), :] * scale).astype(BF16)
+        outs[3][...] = dv_acc[pl.ds(0, tokens), :].astype(BF16)
+        return
     for ref, place in zip(outs[pieces:], range(shards - 2, -1, -1)):
         span = pl.ds(place * tokens, tokens)
         ref[pl.ds(0, tokens), :] = (dk_acc[span, :] * scale).astype(BF16)
@@ -245,7 +249,7 @@
         out_span = pl.ds(index * size % whole, size)
         total = straight_ref[span, :].astype(F32) + ref[...].astype(F32)
         out_refs[index * size // whole][out_span, :] = total.astype(BF16)
-    if outs == 1:
+    if out_refs[0].shape[0] > whole:
         span = pl.ds(whole, SPARE)
         out_refs[0][span, :] = jnp.zeros((SPARE, straight_ref.shape[1]), BF16)
 
@@ -335,10 +339,10 @@
                 shards_kernel, scale=scale, parts=len(parts), shards=shards, place_of=place_of
             ),
             in_specs=[smem] * 3 + [vmem] * (5 + len(parts)),
-            out_specs=[vmem] * (shards + 2),
+            out_specs=[vmem] * 5,
             out_shape=[dq_shape]
             + [stacked(1)] * 2
-            + [stacked(2)] * (shards - 1),
+            + [stacked(shards - 1)] * 2,
             scratch_shapes=[narrow, narrow, wide, wide, items],
             input_output_aliases={7: 0},
             compiler_params=params,
@@ -387,14 +391,19 @@
     listed, live, q, g, norm, delta, dq, dk0, dv0 = own_call()
     k2, v2, dq = lax.optimization_barrier((k2, v2, dq))
     dq, *crossed, near, other = shards_call(
-        dq, (pair_swap(kv), k2, v2, pair_swap(k2), pair_swap(v2)), 3, near_place, "near_shards"
+        dq,
+        (pair_swap(kv), k2, v2, pair_swap(k2), pair_swap(v2)),
+        3, near_place, "near_shards",
     )
     (near,) = add_call(near, [pair_swap(x) for x in crossed], [spare_shape], "near_sum")
     near = ring_shift(near, -2)
     kv4, dq = lax.optimization_barrier((kv4, dq))
-    dq, *crossed, far = shards_call(dq, (kv4, pair_swap(kv4)), 2, far_place, "far_shards")
-    far = add_call(far, [pair_swap(x) for x in crossed], [stacked(1)] * 2, "far_sum")
-    far_k, far_v = (ring_shift(part, -4) for part in far)
+    dq, *parts = shards_call(dq, (kv4, pair_swap(kv4)), 2, far_place, "far_shards")
+    crossed, far = parts[:2], parts[2:]
+    far_k, far_v = (
+        ring_shift(add_call(part, [pair_swap(x)], [stacked(1)], "far_sum")[0], -4)
+        for part, x in zip(far, crossed)
+    )
     near, dq = lax.optimization_barrier((near, dq))
     query_grad = finish_call(dq)
     far_k, far_v, query_grad = lax.optimization_barrier((far_k, far_v, query_grad))

time: 51.4 us -> 51.1 us (level)
  the two profiles are of different devices: /device:TPU:32 before, /device:TPU:1 now
where the time goes in v2:
time: 51.1 us; the launch traced here: 51.6 us
  starting transfers between devices  22.1 us (43%)
  Pallas kernels  15.5 us (30%)
  waiting for transfers between devices  12.5 us (24%)
  other arithmetic  0.83 us (2%)
  between operations  0.71 us (1%)
    ppermute x6, starting transfers between devices, ring_shift(): return lax.ppermute(block, AXES, route)  15.8 us
    ppermute x6, waiting for transfers between devices, ring_shift(): return lax.ppermute(block, AXES, route)  10 us
    pallas_call x1, Pallas kernels, own_call(): pl.pallas_call(functools.partial(own_kernel, scale=scale), in_specs=[smem...  6.71 us
    ppermute x9, starting transfers between devices, pair_swap(): return lax.ppermute(block, AXES, [(i, i ^ 1) for i in range(count)])  6.33 us
    pallas_call x2, Pallas kernels, shards_call(): pl.pallas_call(functools.partial(shards_kernel, scale=scale, parts=len(pa...  5.78 us
    ppermute x9, waiting for transfers between devices, pair_swap(): return lax.ppermute(block, AXES, [(i, i ^ 1) for i in range(count)])  2.5 us
    pallas_call x1, Pallas kernels, finish_call(): pl.pallas_call(functools.partial(finish_kernel, scale=scale), grid=(local...  1.83 us
  transfers between devices with their start and end apart: 15, of which 8 were waited for; matrix products, arithmetic and copies ran while one was open for 0% of the time, Pallas kernels for 30%

profile of v2, /device:TPU:1, one launch (start us, length us, event | category | flops | bytes accessed | tf_op | source)
XLA Modules:
  0.0 51.6 jit_solution(13437152766744832808)
XLA Ops:
  0.6 2.5 %collective-permute-start.1 = (bf16[512,128]{1,0:T(8,128)(2,1)}, bf16[512,128]{1,0:T(8,128)(2,1)S(1)}, u32[]{:S(2)}, u32[]{:S(2)}) collective-permute-start(bf16[512,128]{1,0:T(8,128)(2,1)} %k_hbm.1), channel_id=1, source_target_pairs={{0,2},{1,3},{2,4},{3,5},{4,6},{5,7},{6,8},{7,9},{8,10},{9,11},{10,... | collective-permute-start | bytes 393224 | tf_op jit(solution)/shard_map/ppermute | solution.py:25
  3.2 1.6 %collective-permute-start.2 = (bf16[512,128]{1,0:T(8,128)(2,1)}, bf16[512,128]{1,0:T(8,128)(2,1)S(1)}, u32[]{:S(2)}, u32[]{:S(2)}) collective-permute-start(bf16[512,128]{1,0:T(8,128)(2,1)} %v_hbm.1), channel_id=1, source_target_pairs={{0,2},{1,3},{2,4},{3,5},{4,6},{5,7},{6,8},{7,9},{8,10},{9,11},{10,... | collective-permute-start | bytes 393224 | tf_op jit(solution)/shard_map/ppermute | solution.py:25
  4.8 1.0 %stack.1.both_ref = bf16[1024,128]{1,0:T(8,128)(2,1)S(1)} custom-call(bf16[512,128]{1,0:T(8,128)(2,1)} %k_hbm.1, bf16[512,128]{1,0:T(8,128)(2,1)} %v_hbm.1), custom_call_target="tpu_custom_call" | custom-call | flops 1 | bytes 1 | tf_op jit(solution)/shard_map/stack/pallas_call | solution.py:365
  5.8 1.3 %collective-permute-start.3 = (bf16[1024,128]{1,0:T(8,128)(2,1)S(1)}, bf16[1024,128]{1,0:T(8,128)(2,1)S(1)}, u32[]{:S(2)}, u32[]{:S(2)}) collective-permute-start(bf16[1024,128]{1,0:T(8,128)(2,1)S(1)} %stack.1.both_ref), channel_id=1, source_target_pairs={{0,1},{1,0},{2,3},{3,2},{4,5},{5,4},{6,7},{7,6},{8,9},{9,8},{10,11... | collective-permute-start | bytes 786440 | tf_op jit(solution)/shard_map/ppermute | solution.py:30
  7.1 1.3 %collective-permute-start = (bf16[1024,128]{1,0:T(8,128)(2,1)S(1)}, bf16[1024,128]{1,0:T(8,128)(2,1)S(1)}, u32[]{:S(2)}, u32[]{:S(2)}) collective-permute-start(bf16[1024,128]{1,0:T(8,128)(2,1)S(1)} %stack.1.both_ref), channel_id=1, source_target_pairs={{0,4},{1,5},{2,6},{3,7},{4,8},{5,9},{6,10},{7,11},{8,12},{9,13},{1... | collective-permute-start | bytes 786440 | tf_op jit(solution)/shard_map/ppermute | solution.py:25
  8.4 6.7 %own_shard.1 = (s32[4,8]{1,0:T(4,128)S(1)}, s32[4]{0:T(128)S(1)}, bf16[4096,128]{1,0:T(8,128)(2,1)S(1)}, bf16[4096,128]{1,0:T(8,128)(2,1)S(1)}, f32[4,1,1024]{2,...) custom-call(s32[1]{0:T(128)} %bitcast.position_ref, ...), custom_call_target="tpu_custom_call" | custom-call | flops 1 | bytes 1 | tf_op jit(solution)/shard_map/own_shard/pallas_call | solution.py:311
  15.2 0.0 collective-permute-done.1.refs_2_
  15.2 2.8 %collective-permute-done.2.refs_3_ = bf16[512,128]{1,0:T(8,128)(2,1)S(1)} collective-permute-done((bf16[512,128]{1,0:T(8,128)(2,1)}, bf16[512,128]{1,0:T(8,128)(2,1)S(1)}, u32[]{:S(2)}, u32[]{:S(2)}) %collective-permute-start.2) | collective-permute-done | bytes 131104 | tf_op jit(solution)/shard_map/ppermute | solution.py:25
  18.0 2.5 %collective-permute-start.4 = (bf16[512,128]{1,0:T(8,128)(2,1)S(1)}, bf16[512,128]{1,0:T(8,128)(2,1)S(1)}, u32[]{:S(2)}, u32[]{:S(2)}) collective-permute-start(bf16[512,128]{1,0:T(8,128)(2,1)S(1)} %collective-permute-done.1.refs_2_), channel_id=1, source_target_pairs={{0,1},{1,0},{2,3},{3,2},{4,5},{5,4},{6,7},{7,6},{8,9},{9,8},{10,11... | collective-permute-start | bytes 393224 | tf_op jit(solution)/shard_map/ppermute | solution.py:30
  20.5 0.0 collective-permute-start.5
  20.5 0.0 collective-permute-done.3.refs_1_
  20.5 1.0 %collective-permute-done.4.refs_4_ = bf16[512,128]{1,0:T(8,128)(2,1)S(1)} collective-permute-done((bf16[512,128]{1,0:T(8,128)(2,1)S(1)}, bf16[512,128]{1,0:T(8,128)(2,1)S(1)}, u32[]{:S(2)}, u32[]{:S(2)}) %collective-permute-start.4) | collective-permute-done | bytes 131104 | tf_op jit(solution)/shard_map/ppermute | solution.py:30
  21.5 0.4 collective-permute-done.5.refs_5_
  21.9 4.8 %near_shards.1 = (f32[4,128,1024]{2,1,0:T(8,128)S(1)}, bf16[512,128]{1,0:T(8,128)(2,1)S(1)}, bf16[512,128]{1,0:T(8,128)(2,1)S(1)}, bf16[1024,128]{1,0:T(8,128)(2,1)S(1)}, bf16[1024,128]{1,0:T(8,128)(2,1)S(1)}) custom-call(s32[1]{0:T(128)} %bitcast.position_ref, s32[4,8]{1,0:T(4,128)S(1)} %get-tuple-element.32.list_ref, ...), custom_call_target="tpu_custom_call", output_to_operand_aliasing={{0}: (7, {})} | custom-call | flops 1 | bytes 1 | tf_op jit(solution)/shard_map/near_shards/pallas_call | solution.py:337
  26.7 0.1 collective-permute-start.11
  26.8 0.5 collective-permute-start.12
  27.3 0.0 collective-permute-done.refs_1_
  27.3 0.7 %collective-permute-start.6 = (bf16[1024,128]{1,0:T(8,128)(2,1)S(1)}, bf16[1024,128]{1,0:T(8,128)(2,1)S(1)}, u32[]{:S(2)}, u32[]{:S(2)}) collective-permute-start(bf16[1024,128]{1,0:T(8,128)(2,1)S(1)} %collective-permute-done.refs_1_), channel_id=1, source_target_pairs={{0,1},{1,0},{2,3},{3,2},{4,5},{5,4},{6,7},{7,6},{8,9},{9,8},{10,11... | collective-permute-start | bytes 786440 | tf_op jit(solution)/shard_map/ppermute | solution.py:30
  28.0 0.1 collective-permute-done.11.refs_0_
  28.1 0.2 collective-permute-done.12.refs_1_
  28.3 0.1 near_sum.1
  28.4 4.2 %collective-permute-start.13 = (bf16[1040,128]{1,0:T(8,128)(2,1)S(1)}, bf16[1040,128]{1,0:T(8,128)(2,1)S(1)}, u32[]{:S(2)}, u32[]{:S(2)}) collective-permute-start(bf16[1040,128]{1,0:T(8,128)(2,1)S(1)} %near_sum.1), channel_id=1, source_target_pairs={{0,254},{1,255},{2,0},{3,1},{4,2},{5,3},{6,4},{7,5},{8,6},{9,7},{1... | collective-permute-start | bytes 798728 | tf_op jit(solution)/shard_map/ppermute | solution.py:25
  32.5 0.6 %collective-permute-start.14 = (bf16[1024,128]{1,0:T(8,128)(2,1)S(1)}, bf16[1024,128]{1,0:T(8,128)(2,1)S(1)}, u32[]{:S(2)}, u32[]{:S(2)}) collective-permute-start(bf16[1024,128]{1,0:T(8,128)(2,1)S(1)} %get-tuple-element.56), channel_id=1, source_target_pairs={{0,1},{1,0},{2,3},{3,2},{4,5},{5,4},{6,7},{7,6},{8,9},{9,8},{10,11... | collective-permute-start | bytes 786440 | tf_op jit(solution)/shard_map/ppermute | solution.py:30
  33.1 0.0 collective-permute-done.6.refs_2_
  33.1 1.0 %far_shards.1 = (f32[4,128,1024]{2,1,0:T(8,128)S(1)}, bf16[512,128]{1,0:T(8,128)(2,1)S(1)}, bf16[512,128]{1,0:T(8,128)(2,1)S(1)}, bf16[512,128]{1,0:T(8,128)(2,1)S(1)}, bf16[512,128]{1,0:T(8,128)(2,1)S(1)}) custom-call(s32[1]{0:T(128)} %bitcast.position_ref, s32[4,8]{1,0:T(4,128)S(1)} %get-tuple-element.32.list_ref, ...), custom_call_target="tpu_custom_call", output_to_operand_aliasing={{0}: (7, {})} | custom-call | flops 1 | bytes 1 | tf_op jit(solution)/shard_map/far_shards/pallas_call | solution.py:337
  34.1 0.1 collective-permute-start.7
  34.2 0.5 collective-permute-start.9
  34.7 0.8 %collective-permute-done.7.refs_0_ = bf16[512,128]{1,0:T(8,128)(2,1)S(1)} collective-permute-done((bf16[512,128]{1,0:T(8,128)(2,1)S(1)}, bf16[512,128]{1,0:T(8,128)(2,1)S(1)}, u32[]{:S(2)}, u32[]{:S(2)}) %collective-permute-start.7) | collective-permute-done | bytes 131104 | tf_op jit(solution)/shard_map/ppermute | solution.py:30
  35.6 0.5 collective-permute-start.8
  36.1 0.0 collective-permute-done.9.refs_0_
  36.1 5.7 %collective-permute-start.10 = (bf16[512,128]{1,0:T(8,128)(2,1)S(1)}, bf16[512,128]{1,0:T(8,128)(2,1)S(1)}, u32[]{:S(2)}, u32[]{:S(2)}) collective-permute-start(bf16[512,128]{1,0:T(8,128)(2,1)S(1)} %far_sum.3), channel_id=1, source_target_pairs={{0,252},{1,253},{2,254},{3,255},{4,0},{5,1},{6,2},{7,3},{8,4},{9,5... | collective-permute-start | bytes 393224 | tf_op jit(solution)/shard_map/ppermute | solution.py:25
  41.8 0.0 collective-permute-done.13
  41.8 1.8 %query_grad.1 = bf16[4096,128]{1,0:T(8,128)(2,1)} custom-call(f32[4,128,1024]{2,1,0:T(8,128)S(1)} %get-tuple-element.53.dq_ref), custom_call_target="tpu_custom_call" | custom-call | flops 1 | bytes 1 | tf_op jit(solution)/shard_map/query_grad/pallas_call | solution.py:377
  43.6 0.0 collective-permute-done.14
  43.6 0.1 convert_add_fusion
  43.7 4.3 %collective-permute-done.8 = bf16[512,128]{1,0:T(8,128)(2,1)S(1)} collective-permute-done((bf16[512,128]{1,0:T(8,128)(2,1)S(1)}, bf16[512,128]{1,0:T(8,128)(2,1)S(1)}, u32[]{:S(2)}, u32[]{:S(2)}) %collective-permute-start.8) | collective-permute-done | bytes 131104 | tf_op jit(solution)/shard_map/ppermute | solution.py:25
  48.0 2.8 %collective-permute-done.10 = bf16[512,128]{1,0:T(8,128)(2,1)S(1)} collective-permute-done((bf16[512,128]{1,0:T(8,128)(2,1)S(1)}, bf16[512,128]{1,0:T(8,128)(2,1)S(1)}, u32[]{:S(2)}, u32[]{:S(2)}) %collective-permute-start.10) | collective-permute-done | bytes 131104 | tf_op jit(solution)/shard_map/ppermute | solution.py:25
  50.8 0.8 %fusion.1 = (bf16[512,128]{1,0:T(8,128)(2,1)}, bf16[512,128]{1,0:T(8,128)(2,1)}) fusion(f32[512,128]{1,0:T(8,128)S(1)} %get-tuple-element.59, f32[1024,128]{1,0:T(8,128)S(1)} %convert_add_fusion, bf16[512,128]{1,0:T(8,128)(2,1)S(1)} %collective-permute-done.10, bf16[512,128]{1,0:T(8,128)(2,1)S(1)} %collective-permute-done.8, f32[512,128]{1,0:T(8,128)S(1)} %get-tuple-element.55), kind=kLoop, calls=%fused_computation.3 | loop fusion | flops 524288 | bytes 1572864 | tf_op jit(solution)/shard_map/convert_element_type | solution.py:412
  (2 shorter events, 0.1 us)
Async XLA Ops:
  0.6 14.6 %collective-permute-start.1 = (bf16[512,128]{1,0:T(8,128)(2,1)}, bf16[512,128]{1,0:T(8,128)(2,1)S(1)}, u32[]{:S(2)}, u32[]{:S(2)}) collective-permute-start(bf16[512,128]{1,0:T(8,128)(2,1)} %k_hbm.1), channel_id=1, source_target_pairs={{0,2},{1,3},{2,4},{3,5},{4,6},{5,7},{6,8},{7,9},{8,10},{9,11},{10,... | collective-permute-start | bytes 393224 | tf_op jit(solution)/shard_map/ppermute | solution.py:25
  3.2 14.8 %collective-permute-start.2 = (bf16[512,128]{1,0:T(8,128)(2,1)}, bf16[512,128]{1,0:T(8,128)(2,1)S(1)}, u32[]{:S(2)}, u32[]{:S(2)}) collective-permute-start(bf16[512,128]{1,0:T(8,128)(2,1)} %v_hbm.1), channel_id=1, source_target_pairs={{0,2},{1,3},{2,4},{3,5},{4,6},{5,7},{6,8},{7,9},{8,10},{9,11},{10,... | collective-permute-start | bytes 393224 | tf_op jit(solution)/shard_map/ppermute | solution.py:25
  5.8 14.7 %collective-permute-start.3 = (bf16[1024,128]{1,0:T(8,128)(2,1)S(1)}, bf16[1024,128]{1,0:T(8,128)(2,1)S(1)}, u32[]{:S(2)}, u32[]{:S(2)}) collective-permute-start(bf16[1024,128]{1,0:T(8,128)(2,1)S(1)} %stack.1.both_ref), channel_id=1, source_target_pairs={{0,1},{1,0},{2,3},{3,2},{4,5},{5,4},{6,7},{7,6},{8,9},{9,8},{10,11... | collective-permute-start | bytes 786440 | tf_op jit(solution)/shard_map/ppermute | solution.py:30
  7.1 20.1 %collective-permute-start = (bf16[1024,128]{1,0:T(8,128)(2,1)S(1)}, bf16[1024,128]{1,0:T(8,128)(2,1)S(1)}, u32[]{:S(2)}, u32[]{:S(2)}) collective-permute-start(bf16[1024,128]{1,0:T(8,128)(2,1)S(1)} %stack.1.both_ref), channel_id=1, source_target_pairs={{0,4},{1,5},{2,6},{3,7},{4,8},{5,9},{6,10},{7,11},{8,12},{9,13},{1... | collective-permute-start | bytes 786440 | tf_op jit(solution)/shard_map/ppermute | solution.py:25
  18.0 3.5 %collective-permute-start.4 = (bf16[512,128]{1,0:T(8,128)(2,1)S(1)}, bf16[512,128]{1,0:T(8,128)(2,1)S(1)}, u32[]{:S(2)}, u32[]{:S(2)}) collective-permute-start(bf16[512,128]{1,0:T(8,128)(2,1)S(1)} %collective-permute-done.1.refs_2_), channel_id=1, source_target_pairs={{0,1},{1,0},{2,3},{3,2},{4,5},{5,4},{6,7},{7,6},{8,9},{9,8},{10,11... | collective-permute-start | bytes 393224 | tf_op jit(solution)/shard_map/ppermute | solution.py:30
  20.5 1.3 %collective-permute-start.5 = (bf16[512,128]{1,0:T(8,128)(2,1)S(1)}, bf16[512,128]{1,0:T(8,128)(2,1)S(1)}, u32[]{:S(2)}, u32[]{:S(2)}) collective-permute-start(bf16[512,128]{1,0:T(8,128)(2,1)S(1)} %collective-permute-done.2.refs_3_), channel_id=1, source_target_pairs={{0,1},{1,0},{2,3},{3,2},{4,5},{5,4},{6,7},{7,6},{8,9},{9,8},{10,11... | collective-permute-start | bytes 393224 | tf_op jit(solution)/shard_map/ppermute | solution.py:30
  26.7 1.4 %collective-permute-start.11 = (bf16[512,128]{1,0:T(8,128)(2,1)S(1)}, bf16[512,128]{1,0:T(8,128)(2,1)S(1)}, u32[]{:S(2)}, u32[]{:S(2)}) collective-permute-start(bf16[512,128]{1,0:T(8,128)(2,1)S(1)} %get-tuple-element.50), channel_id=1, source_target_pairs={{0,1},{1,0},{2,3},{3,2},{4,5},{5,4},{6,7},{7,6},{8,9},{9,8},{10,11... | collective-permute-start | bytes 393224 | tf_op jit(solution)/shard_map/ppermute | solution.py:30
  26.8 1.5 %collective-permute-start.12 = (bf16[512,128]{1,0:T(8,128)(2,1)S(1)}, bf16[512,128]{1,0:T(8,128)(2,1)S(1)}, u32[]{:S(2)}, u32[]{:S(2)}) collective-permute-start(bf16[512,128]{1,0:T(8,128)(2,1)S(1)} %get-tuple-element.51), channel_id=1, source_target_pairs={{0,1},{1,0},{2,3},{3,2},{4,5},{5,4},{6,7},{7,6},{8,9},{9,8},{10,11... | collective-permute-start | bytes 393224 | tf_op jit(solution)/shard_map/ppermute | solution.py:30
  27.3 5.8 %collective-permute-start.6 = (bf16[1024,128]{1,0:T(8,128)(2,1)S(1)}, bf16[1024,128]{1,0:T(8,128)(2,1)S(1)}, u32[]{:S(2)}, u32[]{:S(2)}) collective-permute-start(bf16[1024,128]{1,0:T(8,128)(2,1)S(1)} %collective-permute-done.refs_1_), channel_id=1, source_target_pairs={{0,1},{1,0},{2,3},{3,2},{4,5},{5,4},{6,7},{7,6},{8,9},{9,8},{10,11... | collective-permute-start | bytes 786440 | tf_op jit(solution)/shard_map/ppermute | solution.py:30
  28.4 13.4 %collective-permute-start.13 = (bf16[1040,128]{1,0:T(8,128)(2,1)S(1)}, bf16[1040,128]{1,0:T(8,128)(2,1)S(1)}, u32[]{:S(2)}, u32[]{:S(2)}) collective-permute-start(bf16[1040,128]{1,0:T(8,128)(2,1)S(1)} %near_sum.1), channel_id=1, source_target_pairs={{0,254},{1,255},{2,0},{3,1},{4,2},{5,3},{6,4},{7,5},{8,6},{9,7},{1... | collective-permute-start | bytes 798728 | tf_op jit(solution)/shard_map/ppermute | solution.py:25
  32.5 11.1 %collective-permute-start.14 = (bf16[1024,128]{1,0:T(8,128)(2,1)S(1)}, bf16[1024,128]{1,0:T(8,128)(2,1)S(1)}, u32[]{:S(2)}, u32[]{:S(2)}) collective-permute-start(bf16[1024,128]{1,0:T(8,128)(2,1)S(1)} %get-tuple-element.56), channel_id=1, source_target_pairs={{0,1},{1,0},{2,3},{3,2},{4,5},{5,4},{6,7},{7,6},{8,9},{9,8},{10,11... | collective-permute-start | bytes 786440 | tf_op jit(solution)/shard_map/ppermute | solution.py:30
  34.1 1.4 %collective-permute-start.7 = (bf16[512,128]{1,0:T(8,128)(2,1)S(1)}, bf16[512,128]{1,0:T(8,128)(2,1)S(1)}, u32[]{:S(2)}, u32[]{:S(2)}) collective-permute-start(bf16[512,128]{1,0:T(8,128)(2,1)S(1)} %get-tuple-element.46), channel_id=1, source_target_pairs={{0,1},{1,0},{2,3},{3,2},{4,5},{5,4},{6,7},{7,6},{8,9},{9,8},{10,11... | collective-permute-start | bytes 393224 | tf_op jit(solution)/shard_map/ppermute | solution.py:30
  34.2 1.9 %collective-permute-start.9 = (bf16[512,128]{1,0:T(8,128)(2,1)S(1)}, bf16[512,128]{1,0:T(8,128)(2,1)S(1)}, u32[]{:S(2)}, u32[]{:S(2)}) collective-permute-start(bf16[512,128]{1,0:T(8,128)(2,1)S(1)} %get-tuple-element.48), channel_id=1, source_target_pairs={{0,1},{1,0},{2,3},{3,2},{4,5},{5,4},{6,7},{7,6},{8,9},{9,8},{10,11... | collective-permute-start | bytes 393224 | tf_op jit(solution)/shard_map/ppermute | solution.py:30
  35.6 12.4 %collective-permute-start.8 = (bf16[512,128]{1,0:T(8,128)(2,1)S(1)}, bf16[512,128]{1,0:T(8,128)(2,1)S(1)}, u32[]{:S(2)}, u32[]{:S(2)}) collective-permute-start(bf16[512,128]{1,0:T(8,128)(2,1)S(1)} %far_sum.2), channel_id=1, source_target_pairs={{0,252},{1,253},{2,254},{3,255},{4,0},{5,1},{6,2},{7,3},{8,4},{9,5... | collective-permute-start | bytes 393224 | tf_op jit(solution)/shard_map/ppermute | solution.py:25
  36.1 14.7 %collective-permute-start.10 = (bf16[512,128]{1,0:T(8,128)(2,1)S(1)}, bf16[512,128]{1,0:T(8,128)(2,1)S(1)}, u32[]{:S(2)}, u32[]{:S(2)}) collective-permute-start(bf16[512,128]{1,0:T(8,128)(2,1)S(1)} %far_sum.3), channel_id=1, source_target_pairs={{0,252},{1,253},{2,254},{3,255},{4,0},{5,1},{6,2},{7,3},{8,4},{9,5... | collective-permute-start | bytes 393224 | tf_op jit(solution)/shard_map/ppermute | solution.py:25
